TPU v7x, 32 devices: a whole 2x2x4 slice. The times are simulated.
32 devices in a mesh: section: 2 (over x), dp: 16 (over z, y, core).
Axes of the slice: x: 2, y: 2, z: 4, core: 2. Of those that a mesh axis runs over, the one named last changes fastest.
Arguments:
- edge_rows: bfloat16 [2, 4096, 768], P('section', 'dp'), may hold values from -24 to 24
- lengths: int32 [32, 3], P('dp'), may hold values from 1 to 64, 128 in all within a row
- routes: int32 [2, 4096, 1], P('section', 'dp'), may hold values from 0 to 7; in each aligned block of 128 rows (0 to 127, 128 to 255, ..., all dimensions but the last counted through in order) at most 32 rows name the same one
- norm_gains: bfloat16 [2, 2, 768], P('section', None, 'dp'), may hold values from 0.5 to 1.5
- qkv_weight: bfloat16 [2, 768, 2304], P('section', 'dp'), may hold values from -0.21875 to 0.21875
- out_weight: bfloat16 [2, 768, 768], P('section', 'dp'), may hold values from -0.875 to 0.875
- router_weight: bfloat16 [2, 768, 8], P('section', 'dp'), may hold values from -0.109375 to 0.109375
- bias_table: bfloat16 [2, 384], P('section', 'dp'), may hold values from -4 to 4
- expert_in: bfloat16 [2, 768, 24576], P('section', None, 'dp'), may hold values from -0.21875 to 0.21875
- expert_out: bfloat16 [2, 24576, 768], P('section', 'dp'), may hold values from -0.875 to 0.875
Outputs:
- edge_results: float32 [2, 4096, 768], P('section', 'dp')
- grad_gains: float32 [2, 2, 768], P('section', None, 'dp')
- grad_qkv: float32 [2, 768, 2304], P('section', 'dp')
- grad_out: float32 [2, 768, 768], P('section', 'dp')
- grad_router: float32 [2, 768, 8], P('section', 'dp')
- grad_table: float32 [2, 384], P('section', 'dp')
- grad_expert_in: float32 [2, 768, 24576], P('section', None, 'dp')
- grad_expert_out: float32 [2, 24576, 768], P('section', 'dp')
Inputs may be any that keep to these rules, and one draw needn't show every extreme that they name: Each block of 128 tokens holds 3 sequences whose lengths sum to 128; the longest of each block has exactly 64 tokens. `routes`: among the 128 tokens of one block at most 32 name the same expert, and in some blocks an expert is named by exactly 32.
All inputs are finite; a program needn't handle non-finite values.
Results may differ from a plain program's by a relative error of at most 0.019.
Values may be sent and summed in bfloat16 or wider, within the bound.
No kernel may reach another device: no remote copies, remote signals or barrier semaphores. Data moves between devices by JAX's collectives and lax.ppermute only.
A program may use at most 192 MiB of HBM per device.

v0:
```python
import jax
import jax.numpy as jnp
from jax import lax
from jax.sharding import PartitionSpec as P

D = 768
HEADS = 12
HEAD_DIM = 64
BUCKETS = 32
SLOT = 128
MICRO = 2


norm_eps = 1e-06
masked_score = -1e30
bucket_edges = (1, 2, 3, 4, 5, 6, 7, 8, 12, 16, 23, 32, 46, 64, 91)


def from_behind(block, axis, distance):
    devices = range(lax.axis_size(axis))
    route = [(i - distance, i) for i in devices if i - distance in devices]
    return lax.ppermute(block, axis, route)


def rms_scale(values):
    return lax.rsqrt(jnp.mean(values * values, axis=-1, keepdims=True) + norm_eps)


def norm_backward(grad_normed, values, gain_row):
    inv_rms = rms_scale(values)
    weighted = grad_normed * gain_row
    grad_gain = jnp.sum(grad_normed * values * inv_rms, axis=0)
    grad_values = inv_rms * weighted - values * inv_rms**3 * jnp.mean(
        weighted * values, axis=-1, keepdims=True
    )
    return (grad_values, grad_gain)


def bucket_onehot():
    places = jnp.arange(SLOT, dtype=jnp.int32)
    offset = places[None, :] - places[:, None]
    distance = jnp.abs(offset)
    bucket = jnp.zeros_like(distance)
    for threshold in bucket_edges:
        bucket = bucket + (distance >= threshold).astype(jnp.int32)
    bucket = bucket + BUCKETS // 2 * (offset > 0).astype(jnp.int32)
    return (bucket[:, :, None] == jnp.arange(BUCKETS, dtype=jnp.int32)).astype(jnp.bfloat16)


def same_sequence(lengths):
    bounds = jnp.cumsum(lengths, axis=-1)
    places = jnp.arange(SLOT, dtype=jnp.int32)
    owners = jnp.sum((places[:, None] >= bounds[:, None, :]).astype(jnp.int32), axis=-1)
    return owners[:, :, None] == owners[:, None, :]


def expert_places(route_ids, experts, capacity):
    choose = (route_ids[:, None] == jnp.arange(experts, dtype=jnp.int32)[None, :]).astype(jnp.int32)
    before = jnp.cumsum(choose, axis=0) - choose
    rank_ids = jnp.sum(before * choose, axis=-1)
    targets = route_ids * capacity + rank_ids
    placing = (targets[:, None] == jnp.arange(experts * capacity, dtype=jnp.int32)[None, :]).astype(
        jnp.bfloat16
    )
    return (choose.astype(jnp.float32), targets, placing)


def fill_slots(row_data, placing, devices):
    packed = jnp.einsum("ts,td->sd", placing, row_data, preferred_element_type=jnp.float32).astype(
        jnp.bfloat16
    )
    packed = packed.reshape(devices // 2, 1, -1, D)
    return jnp.broadcast_to(packed, (devices // 2, 2) + packed.shape[2:]).reshape(devices, -1, D)


def gather_slots(returned, targets, devices):
    summed = returned.astype(jnp.float32).reshape(devices // 2, 2, -1, D).sum(axis=1).reshape(-1, D)
    return jnp.take(summed, targets, axis=0)


def reply_back(replies):
    return lax.all_to_all(replies, "dp", split_axis=0, concat_axis=0, tiled=True)


def score_block(projected, relative, same_seq):
    scores = (
        jnp.einsum(
            "qhd,khd->hqk", projected[:, 0], projected[:, 1], preferred_element_type=jnp.float32
        )
        * HEAD_DIM ** (-0.5)
        + relative
    )
    return jnp.where(same_seq[None], scores, masked_score)


def layer_forward(inputs, dense_now, relative, same_seq, route_ids, weight_in, weight_out, devices):
    gain_rows, qkv_w, out_w, router_w = dense_now
    extent = inputs.shape[0]
    normed = (inputs * rms_scale(inputs) * gain_rows[0].astype(jnp.float32)).astype(jnp.bfloat16)
    projected = (
        jnp.dot(normed, qkv_w, preferred_element_type=jnp.float32)
        .astype(jnp.bfloat16)
        .reshape(extent, 3, HEADS, HEAD_DIM)
    )
    scores = score_block(projected, relative, same_seq)
    top_score = jnp.max(scores, axis=-1, keepdims=True)
    log_total = top_score + jnp.log(jnp.sum(jnp.exp(scores - top_score), axis=-1, keepdims=True))
    weights = jnp.exp(scores - log_total).astype(jnp.bfloat16)
    attended = (
        jnp.einsum("hqk,khd->qhd", weights, projected[:, 2], preferred_element_type=jnp.float32)
        .astype(jnp.bfloat16)
        .reshape(extent, D)
    )
    middle = inputs + jnp.dot(attended, out_w, preferred_element_type=jnp.float32)
    routed = (middle * rms_scale(middle) * gain_rows[1].astype(jnp.float32)).astype(jnp.bfloat16)
    logits = jnp.dot(routed, router_w, preferred_element_type=jnp.float32)
    route_probs = jax.nn.softmax(logits, axis=-1)
    capacity = 4 * SLOT // devices
    choose, targets, placing = expert_places(route_ids, devices // 2, capacity)
    gate_prob = jnp.sum(route_probs * choose, axis=-1)
    outgoing = fill_slots(routed, placing, devices)
    arrived = lax.all_to_all(outgoing, "dp", split_axis=0, concat_axis=0, tiled=True)
    flat_rows = arrived.reshape(-1, D)
    hidden = jnp.dot(flat_rows, weight_in, preferred_element_type=jnp.float32)
    active = jax.nn.gelu(hidden).astype(jnp.bfloat16)
    replies = jnp.dot(active, weight_out, preferred_element_type=jnp.float32).astype(jnp.bfloat16)
    replies, hidden, arrived = (
        replies.reshape(arrived.shape),
        hidden.reshape(arrived.shape[:2] + (hidden.shape[-1],)),
        arrived,
    )
    result = gather_slots(reply_back(replies), targets, devices)
    outputs = middle + gate_prob[:, None] * result
    kept_now = (
        inputs,
        normed,
        projected,
        log_total,
        attended,
        middle,
        routed,
        route_probs,
        gate_prob,
        result,
        arrived,
        hidden,
    )
    return (outputs, kept_now)


def layer_backward(
    grad_out,
    kept_now,
    dense_now,
    relative,
    same_seq,
    route_ids,
    onehot,
    weight_in,
    weight_out,
    devices,
):
    (
        inputs,
        normed,
        projected,
        log_total,
        attended,
        middle,
        routed,
        route_probs,
        gate_prob,
        result,
        arrived,
        hidden,
    ) = kept_now
    gain_rows, qkv_w, out_w, router_w = dense_now
    extent = inputs.shape[0]
    capacity = 4 * SLOT // devices
    choose, targets, placing = expert_places(route_ids, devices // 2, capacity)
    grad_gate = jnp.sum(grad_out * result, axis=-1)
    grad_result = (gate_prob[:, None] * grad_out).astype(jnp.bfloat16)
    grad_arrived = lax.all_to_all(
        fill_slots(grad_result, placing, devices), "dp", split_axis=0, concat_axis=0, tiled=True
    )
    grad_rows = grad_arrived.reshape(-1, D)
    hidden_rows = hidden.reshape(-1, hidden.shape[-1])
    arrived_rows = arrived.reshape(-1, D)
    active, gelu_pull = jax.vjp(jax.nn.gelu, hidden_rows)
    grad_expert_out = jnp.einsum(
        "rf,rd->fd", active.astype(jnp.bfloat16), grad_rows, preferred_element_type=jnp.float32
    )
    grad_active = jnp.einsum("rd,fd->rf", grad_rows, weight_out, preferred_element_type=jnp.float32)
    grad_hidden = gelu_pull(grad_active)[0].astype(jnp.bfloat16)
    grad_expert_in = jnp.einsum(
        "rd,rf->df", arrived_rows, grad_hidden, preferred_element_type=jnp.float32
    )
    grad_sent = jnp.einsum(
        "rf,df->rd", grad_hidden, weight_in, preferred_element_type=jnp.float32
    ).astype(jnp.bfloat16)
    grad_routed = gather_slots(reply_back(grad_sent.reshape(grad_arrived.shape)), targets, devices)
    grad_logits = ((grad_gate * gate_prob)[:, None] * (choose - route_probs)).astype(jnp.bfloat16)
    grad_router = jnp.einsum("td,te->de", routed, grad_logits, preferred_element_type=jnp.float32)
    grad_routed = grad_routed + jnp.einsum(
        "te,de->td", grad_logits, router_w, preferred_element_type=jnp.float32
    )
    grad_middle_norm, grad_gain_two = norm_backward(
        grad_routed, middle, gain_rows[1].astype(jnp.float32)
    )
    grad_middle = grad_out + grad_middle_norm
    grad_branch = grad_middle.astype(jnp.bfloat16)
    grad_out_w = jnp.einsum("tf,td->fd", attended, grad_branch, preferred_element_type=jnp.float32)
    grad_attended = (
        jnp.einsum("td,fd->tf", grad_branch, out_w, preferred_element_type=jnp.float32)
        .astype(jnp.bfloat16)
        .reshape(extent, HEADS, HEAD_DIM)
    )
    scores = score_block(projected, relative, same_seq)
    attn_probs = jnp.exp(scores - log_total)
    grad_values = jnp.einsum(
        "hqk,qhd->khd",
        attn_probs.astype(jnp.bfloat16),
        grad_attended,
        preferred_element_type=jnp.float32,
    )
    grad_probs = jnp.einsum(
        "qhd,khd->hqk", grad_attended, projected[:, 2], preferred_element_type=jnp.float32
    )
    grad_scores = (
        attn_probs * (grad_probs - jnp.sum(attn_probs * grad_probs, axis=-1, keepdims=True))
    ).astype(jnp.bfloat16)
    scale_qk = HEAD_DIM ** (-0.5)
    grad_queries = (
        jnp.einsum("hqk,khd->qhd", grad_scores, projected[:, 1], preferred_element_type=jnp.float32)
        * scale_qk
    )
    grad_keys = (
        jnp.einsum("hqk,qhd->khd", grad_scores, projected[:, 0], preferred_element_type=jnp.float32)
        * scale_qk
    )
    grad_table = jnp.einsum(
        "hqk,qkb->bh", grad_scores, onehot, preferred_element_type=jnp.float32
    ).reshape(-1)
    grad_projected = (
        jnp.stack([grad_queries, grad_keys, grad_values], axis=1)
        .astype(jnp.bfloat16)
        .reshape(extent, 3 * D)
    )
    grad_qkv = jnp.einsum("td,tf->df", normed, grad_projected, preferred_element_type=jnp.float32)
    grad_normed = jnp.einsum("tf,df->td", grad_projected, qkv_w, preferred_element_type=jnp.float32)
    grad_inputs_norm, grad_gain_one = norm_backward(
        grad_normed, inputs, gain_rows[0].astype(jnp.float32)
    )
    grad_inputs = grad_middle + grad_inputs_norm
    dense_grads = (
        jnp.stack([grad_gain_one, grad_gain_two]),
        grad_qkv,
        grad_out_w,
        grad_router,
        grad_table,
    )
    return (grad_inputs, dense_grads, (grad_expert_in, grad_expert_out))


def select_section(condition, first_tree, second_tree):
    return jax.tree.map(
        lambda first_leaf, second_leaf: jnp.where(condition, first_leaf, second_leaf),
        first_tree,
        second_tree,
    )


def shards(
    edge_rows,
    lengths,
    routes,
    norm_gains,
    qkv_weight,
    out_weight,
    router_weight,
    bias_table,
    expert_in,
    expert_out,
):
    devices = lax.axis_size("dp")
    first_section = lax.axis_index("section") == 0
    local_rows = edge_rows[0].reshape(MICRO, SLOT, D)
    route_rows = routes[0, :, 0].reshape(MICRO, SLOT)
    same_all = same_sequence(lengths)
    onehot = bucket_onehot()
    weight_in = expert_in[0]
    weight_out = expert_out[0]
    local_dense = (norm_gains[0], qkv_weight[0], out_weight[0], router_weight[0], bias_table[0])
    gathered = (
        lax.all_gather(local_dense[0], "dp", axis=1, tiled=True),
        lax.all_gather(local_dense[1], "dp", axis=0, tiled=True),
        lax.all_gather(local_dense[2], "dp", axis=0, tiled=True),
        lax.all_gather(local_dense[3], "dp", axis=0, tiled=True),
        lax.all_gather(local_dense[4], "dp", axis=0, tiled=True),
    )
    fetch_relative = jnp.einsum(
        "qkb,bh->hqk",
        onehot,
        gathered[4].reshape(BUCKETS, HEADS),
        preferred_element_type=jnp.float32,
    )
    held_dense = (gathered[:4], fetch_relative)
    carried = jnp.zeros((SLOT, D), jnp.bfloat16)
    turn_outputs = []
    turn_saved = []
    for turn_id in range(MICRO + 1):
        dense_now, relative = held_dense
        early_id = min(turn_id, MICRO - 1)
        late_id = max(turn_id - 1, 0)
        inputs = jnp.where(
            first_section, local_rows[early_id].astype(jnp.float32), carried.astype(jnp.float32)
        )
        route_ids = jnp.where(first_section, route_rows[early_id], route_rows[late_id])
        same_seq = jnp.where(first_section, same_all[early_id], same_all[late_id])
        outputs, kept_now = layer_forward(
            inputs, dense_now, relative, same_seq, route_ids, weight_in, weight_out, devices
        )
        turn_outputs.append(outputs)
        turn_saved.append(kept_now)
        if turn_id < MICRO:
            carried = from_behind(outputs.astype(jnp.bfloat16), "section", 1)
    kept_list = [
        select_section(first_section, turn_saved[micro_id], turn_saved[micro_id + 1])
        for micro_id in range(MICRO)
    ]
    dense_total = (
        jnp.zeros((2, D), jnp.float32),
        jnp.zeros((D, 3 * D), jnp.float32),
        jnp.zeros((D, D), jnp.float32),
        jnp.zeros((D, devices // 2), jnp.float32),
        jnp.zeros((BUCKETS * HEADS,), jnp.float32),
    )
    expert_total = (
        jnp.zeros(weight_in.shape, jnp.float32),
        jnp.zeros(weight_out.shape, jnp.float32),
    )
    incoming = jnp.zeros((SLOT, D), jnp.bfloat16)
    input_grads = []
    for turn_id in range(MICRO + 1):
        dense_now, relative = held_dense
        early_id = min(turn_id, MICRO - 1)
        late_id = max(turn_id - 1, 0)
        grad_out = jnp.where(
            first_section, incoming.astype(jnp.float32), local_rows[early_id].astype(jnp.float32)
        )
        kept_now = select_section(first_section, kept_list[late_id], kept_list[early_id])
        route_ids = jnp.where(first_section, route_rows[late_id], route_rows[early_id])
        same_seq = jnp.where(first_section, same_all[late_id], same_all[early_id])
        usable = jnp.where(first_section, turn_id >= 1, turn_id < MICRO).astype(jnp.float32)
        grad_inputs, dense_grads, expert_grads = layer_backward(
            grad_out,
            kept_now,
            dense_now,
            relative,
            same_seq,
            route_ids,
            onehot,
            weight_in,
            weight_out,
            devices,
        )
        dense_grads = jax.tree.map(lambda member: member * usable, dense_grads)
        expert_total = jax.tree.map(
            lambda first_leaf, second_leaf: first_leaf + second_leaf * usable,
            expert_total,
            expert_grads,
        )
        dense_total = jax.tree.map(
            lambda first_leaf, second_leaf: first_leaf + second_leaf, dense_total, dense_grads
        )
        input_grads.append(grad_inputs)
        if turn_id < MICRO:
            incoming = from_behind(grad_inputs.astype(jnp.bfloat16), "section", -1)
    ends_rows = [
        jnp.where(first_section, input_grads[micro_id + 1], turn_outputs[micro_id + 1])
        for micro_id in range(MICRO)
    ]
    edge_results = jnp.stack(ends_rows).reshape(1, MICRO * SLOT, D)
    return (
        edge_results,
        lax.psum_scatter(dense_total[0], "dp", scatter_dimension=1, tiled=True)[None],
        lax.psum_scatter(dense_total[1], "dp", scatter_dimension=0, tiled=True)[None],
        lax.psum_scatter(dense_total[2], "dp", scatter_dimension=0, tiled=True)[None],
        lax.psum_scatter(dense_total[3], "dp", scatter_dimension=0, tiled=True)[None],
        lax.psum_scatter(dense_total[4], "dp", scatter_dimension=0, tiled=True)[None],
        expert_total[0][None],
        expert_total[1][None],
    )


def solution(mesh):
    return jax.shard_map(
        shards,
        mesh=mesh,
        in_specs=(
            P("section", "dp", None),
            P("dp", None),
            P("section", "dp", None),
            P("section", None, "dp"),
            P("section", "dp", None),
            P("section", "dp", None),
            P("section", "dp", None),
            P("section", "dp"),
            P("section", None, "dp"),
            P("section", "dp", None),
        ),
        out_specs=(
            P("section", "dp", None),
            P("section", None, "dp"),
            P("section", "dp", None),
            P("section", "dp", None),
            P("section", "dp", None),
            P("section", "dp"),
            P("section", None, "dp"),
            P("section", "dp", None),
        ),
        check_vma=False,
    )
```

profile of v0, /device:TPU:0, one launch (start us, length us, event | category | flops | bytes accessed | tf_op | source)
XLA Modules:
  0.0 836.5 jit_solution(4803044355499894850)
XLA Ops:
  13.3 35.3 %all-reduce = bf16[384]{0:T(512)(128)(2,1)S(1)} all-reduce(bf16[384]{0:T(512)(128)(2,1)S(1)} %dynamic-update-slice), channel_id=4, replica_groups=mesh['section'=2,'dp'=16] {'dp'}, use_global_device_ids=true, to_apply=%add | all-reduce | flops 384 | bytes 1536
  51.2 18.9 %all-gather = bf16[1,2,768]{1,0,2:T(2,128)(2,1)S(1)} all-gather(bf16[1,2,48]{1,0,2:T(2,128)(2,1)S(1)} %copy.198), channel_id=2, replica_groups=mesh['section'=2,'dp'=16] {'dp'}, dimensions={2}, use_global_device_ids=true | all-gather | bytes 3264 | tf_op jit(solution)/shard_map/all_gather | solution.py:295
  70.1 4.6 fusion.215
  84.0 3.5 convolution_convert_fusion.2
  93.6 8.1 all-gather.10.cloned.1.call-done
  105.2 24.2 %all_to_all.60 = bf16[16,32,768]{2,1,0:T(8,128)(2,1)S(1)} all-to-all(bf16[16,32,768]{2,1,0:T(8,128)(2,1)S(1)} %bitcast.506), channel_id=1, replica_groups=mesh['section'=2,'dp'=16] {'dp'}, dimensions={0} | all-to-all | bytes 1572864 | tf_op jit(solution)/shard_map/all_to_all | solution.py:122
  134.8 4.3 all-to-all-start.1
  144.8 26.5 %all-gather.4 = bf16[1,768,8]{2,0,1:T(2,128)(2,1)} all-gather(bf16[1,48,8]{2,0,1:T(2,128)(2,1)} %copy.205), channel_id=6, replica_groups=mesh['section'=2,'dp'=16] {'dp'}, dimensions={1}, use_global_device_ids=true | all-gather | bytes 13056 | tf_op jit(solution)/shard_map/all_gather | solution.py:298
  184.7 3.4 collective-permute-start
  189.4 3.4 collective-permute-done
  194.2 3.5 convolution_convert_fusion.1
  204.8 24.2 %all_to_all.61 = bf16[16,32,768]{2,1,0:T(8,128)(2,1)S(1)} all-to-all(bf16[16,32,768]{2,1,0:T(8,128)(2,1)S(1)} %bitcast.507), channel_id=1, replica_groups=mesh['section'=2,'dp'=16] {'dp'}, dimensions={0} | all-to-all | bytes 1572864 | tf_op jit(solution)/shard_map/all_to_all | solution.py:122
  234.4 4.3 all-to-all-start.5
  243.5 13.9 %all-to-all-done.5 = bf16[16,32,768]{2,1,0:T(8,128)(2,1)} async-done(((bf16[16,32,768]{2,1,0:T(8,128)(2,1)}), bf16[16,32,768]{2,1,0:T(8,128)(2,1)}, u32[]{:S(2)}, u32[]{:S(2)}) %all-to-all-start.5) | async-done | bytes 786464 | tf_op jit(solution)/shard_map/all_to_all | solution.py:82
  264.0 4.6 collective-permute-start.2
  268.6 4.4 collective-permute-done.2
  289.8 5.5 all-to-all-start.7
  305.8 8.3 all-to-all-done.7
  316.0 5.5 all-to-all-start.2
  327.0 8.3 broadcast_select_fusion.1
  335.3 5.0 all-to-all-done.2
  340.3 5.7 fusion.15
  348.4 5.5 all-to-all-start.4
  363.4 9.3 %all-to-all-done.4 = bf16[16,32,768]{2,1,0:T(8,128)(2,1)} async-done(((bf16[16,32,768]{2,1,0:T(8,128)(2,1)}), bf16[16,32,768]{2,1,0:T(8,128)(2,1)}, u32[]{:S(2)}, u32[]{:S(2)}) %all-to-all-start.4) | async-done | bytes 786464 | tf_op jit(solution)/shard_map/all_to_all | solution.py:82
  372.7 5.8 all-to-all-start.9
  404.2 3.0 gather_fusion.4
  414.1 25.8 %all_to_all.62 = bf16[16,32,768]{2,1,0:T(8,128)(2,1)S(1)} all-to-all(bf16[16,32,768]{2,1,0:T(8,128)(2,1)S(1)} %bitcast.508), channel_id=1, replica_groups=mesh['section'=2,'dp'=16] {'dp'}, dimensions={0} | all-to-all | bytes 1572864 | tf_op jit(solution)/shard_map/all_to_all | solution.py:183
  439.9 5.5 fusion.22
  447.8 4.7 all-to-all-start.8
  456.3 15.0 %all-to-all-done.8 = bf16[16,32,768]{2,1,0:T(8,128)(2,1)} async-done(((bf16[16,32,768]{2,1,0:T(8,128)(2,1)}), bf16[16,32,768]{2,1,0:T(8,128)(2,1)}, u32[]{:S(2)}, u32[]{:S(2)}) %all-to-all-start.8) | async-done | bytes 786464 | tf_op jit(solution)/shard_map/all_to_all | solution.py:82
  493.0 7.6 collective-permute-done.3
  502.7 5.5 all-to-all-start.10
  516.3 10.7 %all-to-all-done.10 = bf16[16,32,768]{2,1,0:T(8,128)(2,1)} async-done(((bf16[16,32,768]{2,1,0:T(8,128)(2,1)}), bf16[16,32,768]{2,1,0:T(8,128)(2,1)}, u32[]{:S(2)}, u32[]{:S(2)}) %all-to-all-start.10) | async-done | bytes 786464 | tf_op jit(solution)/shard_map/all_to_all | solution.py:183
  527.0 5.7 fusion.29
  535.0 5.5 all-to-all-start.11
  544.8 3.1 fusion.249
  554.7 4.6 all-to-all-done.11
  580.1 4.4 multiply_add_fusion.1
  588.5 4.1 multiply_add_fusion
  595.8 3.6 fusion.343
  599.4 5.2 fusion.87
  605.2 3.6 fusion.344
  608.8 4.1 fusion.88
  614.9 8.3 add_bitcast_fusion.1
  623.2 5.5 add_bitcast_fusion
  629.5 33.5 %all-reduce.1 = f32[384]{0:T(512)S(1)} all-reduce(f32[384]{0:T(512)S(1)} %add.625), channel_id=11, replica_groups=mesh['section'=2,'dp'=16] {'dp'}, use_global_device_ids=true, to_apply=%region_65.67.clone | all-reduce | flops 384 | bytes 3072
  670.5 64.9 %reduce-scatter.11.cloned.1.call-done = f32[48,768]{1,0:T(8,128)} async-done(((f32[768,768]{1,0:T(8,128)}), f32[48,768]{1,0:T(8,128)}) %reduce-scatter.11.cloned.1.call-update) | async-done | bytes 147472 | tf_op jit(solution)/shard_map/reduce_scatter | solution.py:388
  735.4 94.0 %reduce-scatter.9.cloned.1.call-done = f32[48,2304]{1,0:T(8,128)} async-done(((f32[768,2304]{1,0:T(8,128)}), f32[48,2304]{1,0:T(8,128)}) %reduce-scatter.9.cloned.1.call-update) | async-done | bytes 442384 | tf_op jit(solution)/shard_map/reduce_scatter | solution.py:387
  (542 shorter events, 244.7 us)
Async XLA Ops:
  7.2 123.1 %copy-start = (bf16[1,768,1536]{2,1,0:T(8,128)(2,1)S(1)}, bf16[1,768,1536]{2,1,0:T(8,128)(2,1)}, u32[]{:S(2)}) copy-start(bf16[1,768,1536]{2,1,0:T(8,128)(2,1)} %param.20) | copy-start | bytes 7077892
  7.2 76.8 %all-gather.8.cloned.1.call-start = ((), (), s32[]{:S(2)}) async-start(), calls=%async_computation.18 | async-start | bytes 3760128 | tf_op jit(solution)/shard_map/all_gather | solution.py:296
  7.9 93.8 %all-gather.10.cloned.1.call-start = ((), (), s32[]{:S(2)}) async-start(), calls=%async_computation.19 | async-start | bytes 1253376 | tf_op jit(solution)/shard_map/all_gather | solution.py:297
  8.8 65.9 %copy-start.90 = (s32[128,128]{0,1:T(8,128)}, s32[128,128]{0,1:T(8,128)S(1)}, u32[]{:S(2)}) copy-start(s32[128,128]{0,1:T(8,128)S(1)} %select_add_fusion) | copy-start | bytes 196612
  51.2 29.1 %copy-start.5 = (bf16[1,256,768]{2,1,0:T(8,128)(2,1)S(1)}, bf16[1,256,768]{2,1,0:T(8,128)(2,1)}, u32[]{:S(2)}) copy-start(bf16[1,256,768]{2,1,0:T(8,128)(2,1)} %param.12) | copy-start | bytes 1179652
  74.7 28.8 %copy-start.87 = (f32[768]{0:T(1024)}, f32[768]{0:T(1024)S(1)}, u32[]{:S(2)}) copy-start(f32[768]{0:T(1024)S(1)} %get-tuple-element.23) | copy-start | bytes 9220
  81.2 9.8 %copy-start.109 = (f32[128]{0:T(128)}, f32[128]{0:T(128)S(1)}, u32[]{:S(2)}) copy-start(f32[128]{0:T(128)S(1)} %add_rsqrt_fusion.11) | copy-start | bytes 1540
  82.5 22.0 %copy-start.143 = (s32[128]{0:T(128)}, s32[128]{0:T(128)S(1)}, u32[]{:S(2)}) copy-start(s32[128]{0:T(128)S(1)} %get-tuple-element.72) | copy-start | bytes 1540
  132.0 7.9 copy-start.131
  134.8 43.5 %all-to-all-start.1 = ((bf16[16,32,768]{2,1,0:T(8,128)(2,1)}), bf16[16,32,768]{2,1,0:T(8,128)(2,1)}, u32[]{:S(2)}, u32[]{:S(2)}) async-start(bf16[16,32,768]{2,1,0:T(8,128)(2,1)} %bitcast.532), calls=%async_computation.1 | async-start | bytes 1572864 | tf_op jit(solution)/shard_map/all_to_all | solution.py:82
  184.7 8.1 collective-permute-start
  234.4 23.0 %all-to-all-start.5 = ((bf16[16,32,768]{2,1,0:T(8,128)(2,1)}), bf16[16,32,768]{2,1,0:T(8,128)(2,1)}, u32[]{:S(2)}, u32[]{:S(2)}) async-start(bf16[16,32,768]{2,1,0:T(8,128)(2,1)} %bitcast.535), calls=%async_computation.5 | async-start | bytes 1572864 | tf_op jit(solution)/shard_map/all_to_all | solution.py:82
  262.6 15.4 %copy-start.1 = (bf16[1,768,2304]{2,1,0:T(8,128)(2,1)S(1)}, bf16[1,768,2304]{2,1,0:T(8,128)(2,1)}, u32[]{:S(2)}) copy-start(bf16[1,768,2304]{2,1,0:T(8,128)(2,1)} %all-gather.8.cloned.1.call-done) | copy-start | bytes 10616836
  264.0 8.9 %collective-permute-start.2 = (bf16[128,768]{1,0:T(8,128)(2,1)S(1)}, bf16[128,768]{1,0:T(8,128)(2,1)S(1)}, u32[]{:S(2)}, u32[]{:S(2)}) collective-permute-start(bf16[128,768]{1,0:T(8,128)(2,1)S(1)} %fusion.326), channel_id=1, source_target_pairs={{0,16},{1,17},{2,18},{3,19},{4,20},{5,21},{6,22},{7,23},{8,24},{9,... | collective-permute-start | bytes 589832 | tf_op jit(solution)/shard_map/ppermute | solution.py:22
  289.8 24.3 %all-to-all-start.7 = ((bf16[16,32,768]{2,1,0:T(8,128)(2,1)}), bf16[16,32,768]{2,1,0:T(8,128)(2,1)}, u32[]{:S(2)}, u32[]{:S(2)}) async-start(bf16[16,32,768]{2,1,0:T(8,128)(2,1)} %bitcast.504), calls=%async_computation.7 | async-start | bytes 1572864 | tf_op jit(solution)/shard_map/all_to_all | solution.py:122
  316.0 24.3 %all-to-all-start.2 = ((bf16[16,32,768]{2,1,0:T(8,128)(2,1)}), bf16[16,32,768]{2,1,0:T(8,128)(2,1)}, u32[]{:S(2)}, u32[]{:S(2)}) async-start(bf16[16,32,768]{2,1,0:T(8,128)(2,1)} %bitcast.503), calls=%async_computation.2 | async-start | bytes 1572864 | tf_op jit(solution)/shard_map/all_to_all | solution.py:183
  348.4 24.3 %all-to-all-start.4 = ((bf16[16,32,768]{2,1,0:T(8,128)(2,1)}), bf16[16,32,768]{2,1,0:T(8,128)(2,1)}, u32[]{:S(2)}, u32[]{:S(2)}) async-start(bf16[16,32,768]{2,1,0:T(8,128)(2,1)} %bitcast.533), calls=%async_computation.4 | async-start | bytes 1572864 | tf_op jit(solution)/shard_map/all_to_all | solution.py:82
  372.7 29.3 %all-to-all-start.9 = ((bf16[16,32,768]{2,1,0:T(8,128)(2,1)}), bf16[16,32,768]{2,1,0:T(8,128)(2,1)}, u32[]{:S(2)}, u32[]{:S(2)}) async-start(bf16[16,32,768]{2,1,0:T(8,128)(2,1)} %bitcast.529), calls=%async_computation.9 | async-start | bytes 1572864 | tf_op jit(solution)/shard_map/all_to_all | solution.py:82
  400.1 9.7 %collective-permute-start.1 = (bf16[128,768]{1,0:T(8,128)(2,1)}, bf16[128,768]{1,0:T(8,128)(2,1)}, u32[]{:S(2)}, u32[]{:S(2)}) collective-permute-start(bf16[128,768]{1,0:T(8,128)(2,1)} %add_convert_fusion), channel_id=1, source_target_pairs={{16,0},{17,1},{18,2},{19,3},{20,4},{21,5},{22,6},{23,7},{24,8},{25... | collective-permute-start | bytes 589832 | tf_op jit(solution)/shard_map/ppermute | solution.py:22
  407.2 32.7 %copy-start.16 = (f32[512,1536]{1,0:T(8,128)S(1)}, f32[512,1536]{1,0:T(8,128)}, u32[]{:S(2)}) copy-start(f32[512,1536]{1,0:T(8,128)} %get-tuple-element.60) | copy-start | bytes 9437188
  447.8 23.5 %all-to-all-start.8 = ((bf16[16,32,768]{2,1,0:T(8,128)(2,1)}), bf16[16,32,768]{2,1,0:T(8,128)(2,1)}, u32[]{:S(2)}, u32[]{:S(2)}) async-start(bf16[16,32,768]{2,1,0:T(8,128)(2,1)} %bitcast.534), calls=%async_computation.8 | async-start | bytes 1572864 | tf_op jit(solution)/shard_map/all_to_all | solution.py:82
  488.8 12.6 %copy-start.138 = (s32[128]{0:T(128)S(1)}, s32[128]{0:T(128)}, u32[]{:S(2)}) copy-start(s32[128]{0:T(128)} %get-tuple-element.53) | copy-start | bytes 1540
  488.8 12.6 %copy-start.144 = (f32[128]{0:T(128)S(1)}, f32[128]{0:T(128)}, u32[]{:S(2)}) copy-start(f32[128]{0:T(128)} %get-tuple-element.51) | copy-start | bytes 1540
  491.7 8.9 %collective-permute-start.3 = (bf16[128,768]{1,0:T(8,128)(2,1)S(1)}, bf16[128,768]{1,0:T(8,128)(2,1)S(1)}, u32[]{:S(2)}, u32[]{:S(2)}) collective-permute-start(bf16[128,768]{1,0:T(8,128)(2,1)S(1)} %get-tuple-element.29), channel_id=1, source_target_pairs={{16,0},{17,1},{18,2},{19,3},{20,4},{21,5},{22,6},{23,7},{24,8},{25... | collective-permute-start | bytes 589832 | tf_op jit(solution)/shard_map/ppermute | solution.py:22
  502.7 24.3 %all-to-all-start.10 = ((bf16[16,32,768]{2,1,0:T(8,128)(2,1)}), bf16[16,32,768]{2,1,0:T(8,128)(2,1)}, u32[]{:S(2)}, u32[]{:S(2)}) async-start(bf16[16,32,768]{2,1,0:T(8,128)(2,1)} %bitcast.505), calls=%async_computation.10 | async-start | bytes 1572864 | tf_op jit(solution)/shard_map/all_to_all | solution.py:183
  535.0 24.3 %all-to-all-start.11 = ((bf16[16,32,768]{2,1,0:T(8,128)(2,1)}), bf16[16,32,768]{2,1,0:T(8,128)(2,1)}, u32[]{:S(2)}, u32[]{:S(2)}) async-start(bf16[16,32,768]{2,1,0:T(8,128)(2,1)} %bitcast.530), calls=%async_computation.11 | async-start | bytes 1572864 | tf_op jit(solution)/shard_map/all_to_all | solution.py:82
  540.5 72.9 %reduce-scatter.15.cloned.1.call-start = ((), (), s32[]{:S(2)}) async-start(), calls=%async_computation.21 | async-start | bytes 417792
  540.6 7.4 copy-start.69
  540.6 7.4 copy-start.71
  540.6 7.4 copy-start.73
  540.6 7.3 copy-start.93
  540.6 7.3 copy-start.95
  540.6 7.3 copy-start.98
  540.7 7.5 copy-start.106
  540.8 8.1 copy-start.108
  540.8 8.7 %copy-start.32 = (f32[128,768]{1,0:T(8,128)S(1)}, f32[128,768]{1,0:T(8,128)}, u32[]{:S(2)}) copy-start(f32[128,768]{1,0:T(8,128)} %copy-done.30) | copy-start | bytes 1179652
  540.8 8.7 %copy-start.61 = (bf16[128,768]{1,0:T(8,128)(2,1)S(1)}, bf16[128,768]{1,0:T(8,128)(2,1)}, u32[]{:S(2)}) copy-start(bf16[128,768]{1,0:T(8,128)(2,1)} %copy.237) | copy-start | bytes 589828
  540.8 8.7 %copy-start.78 = (bf16[128,768]{1,0:T(8,128)(2,1)S(1)}, bf16[128,768]{1,0:T(8,128)(2,1)}, u32[]{:S(2)}) copy-start(bf16[128,768]{1,0:T(8,128)(2,1)} %copy.239) | copy-start | bytes 589828
  540.8 8.7 %copy-start.79 = (bf16[128,768]{1,0:T(8,128)(2,1)S(1)}, bf16[128,768]{1,0:T(8,128)(2,1)}, u32[]{:S(2)}) copy-start(bf16[128,768]{1,0:T(8,128)(2,1)} %copy.236) | copy-start | bytes 589828
  554.7 114.5 %reduce-scatter.13.cloned.1.call-start = ((), (), s32[]{:S(2)}) async-start(), calls=%async_computation.20 | async-start | bytes 417792
  580.0 155.4 %reduce-scatter.11.cloned.1.call-start = ((), (), s32[]{:S(2)}) async-start(), calls=%async_computation.17 | async-start | bytes 2506752 | tf_op jit(solution)/shard_map/reduce_scatter | solution.py:388
  584.6 244.9 %reduce-scatter.9.cloned.1.call-start = ((), (), s32[]{:S(2)}) async-start(), calls=%async_computation.16 | async-start | bytes 7520256 | tf_op jit(solution)/shard_map/reduce_scatter | solution.py:387
  614.9 8.3 copy-start.18
  614.9 8.3 copy-start.41
  623.2 40.4 %copy-start.28 = (f32[128,768]{1,0:T(8,128)S(1)}, f32[128,768]{1,0:T(8,128)}, u32[]{:S(2)}) copy-start(f32[128,768]{1,0:T(8,128)} %get-tuple-element.31) | copy-start | bytes 1179652
  623.2 40.4 %copy-start.112 = (pred[128]{0:T(512)(128)(4,1)S(1)}, pred[128]{0:T(512)(128)(4,1)}, u32[]{:S(2)}) copy-start(pred[128]{0:T(512)(128)(4,1)} %get-tuple-element.52) | copy-start | bytes 388
  623.2 40.4 %copy-start.136 = (f32[128]{0:T(128)S(1)}, f32[128]{0:T(128)}, u32[]{:S(2)}) copy-start(f32[128]{0:T(128)} %multiply_reduce_fusion.28) | copy-start | bytes 1540
  623.2 40.4 %copy-start.148 = (f32[128]{0:T(128)S(1)}, f32[128]{0:T(128)}, u32[]{:S(2)}) copy-start(f32[128]{0:T(128)} %get-tuple-element.77) | copy-start | bytes 1540
  (126 other events, 397.9 us)
Sparse Core Ops, SparseCore 0:
  10.3 52.4 all-gather.7
  65.1 36.5 all-gather.9
  554.8 55.9 reduce-scatter.14
  614.5 54.5 reduce-scatter.12
  673.3 62.0 reduce-scatter.10
  740.4 89.0 reduce-scatter.8
where the time goes:
time: 848 us; the launch traced here: 836 us
  waiting for transfers between devices  255 us (30%)
  blocking collectives  188 us (22%)
  matrix products  152 us (18%)
  local copies, waits for them, and re-layouts  83.1 us (10%)
  other arithmetic  82.3 us (10%)
  starting transfers between devices  57.6 us (7%)
  between operations  17.6 us (2%)
    reduce_scatter x1, waiting for transfers between devices, shards(): lax.psum_scatter(dense_total[1], 'dp', scatter_dimension=0, tiled=True)  94 us
    unnamed x2, blocking collectives  68.8 us
    reduce_scatter x1, waiting for transfers between devices, shards(): lax.psum_scatter(dense_total[2], 'dp', scatter_dimension=0, tiled=True)  64.9 us
    all_to_all x2, blocking collectives, layer_forward(): lax.all_to_all(outgoing, 'dp', split_axis=0, concat_axis=0, tiled=True)  48.4 us
    all_to_all x6, waiting for transfers between devices, reply_back(): lax.all_to_all(replies, 'dp', split_axis=0, concat_axis=0, tiled=True)  42.7 us
    all_to_all x6, starting transfers between devices, reply_back(): lax.all_to_all(replies, 'dp', split_axis=0, concat_axis=0, tiled=True)  30.1 us
    unnamed x319, local copies, waits for them, and re-layouts  28.4 us
    all_gather x1, blocking collectives, shards(): lax.all_gather(local_dense[3], 'dp', axis=0, tiled=True)  26.5 us
  transfers between devices with their start and end apart: 19, of which 15 were waited for; matrix products, arithmetic and copies ran while one was open for 24% of the time, Pallas kernels for 0%

commit v1 on v0

v1 whole, which is shorter than its diff:
```python
import jax
import jax.numpy as jnp
from jax import lax
from jax.sharding import PartitionSpec as P

D = 768
HEADS = 12
HEAD_DIM = 64
BUCKETS = 32
SLOT = 128


norm_eps = 1e-06
masked_score = -1e30
bucket_edges = (1, 2, 3, 4, 5, 6, 7, 8, 12, 16, 23, 32, 46, 64, 91)
bf16 = jnp.bfloat16
f32 = jnp.float32


def dot(lhs, rhs):
    return jnp.dot(lhs, rhs, preferred_element_type=f32)


def section_shift(block, distance):
    devices = range(lax.axis_size("section"))
    route = [(i - distance, i) for i in devices if i - distance in devices]
    return lax.ppermute(block, "section", route)


def pair_swap(block):
    return lax.ppermute(block, "dp", [(i, i ^ 1) for i in range(lax.axis_size("dp"))])


def chip_all_to_all(block):
    devices = lax.axis_size("dp")
    groups = [list(range(core, devices, 2)) for core in range(2)]
    return lax.all_to_all(
        block, "dp", split_axis=0, concat_axis=0, tiled=True, axis_index_groups=groups
    )


def rms_scale(values):
    return lax.rsqrt(jnp.mean(values * values, axis=-1, keepdims=True) + norm_eps)


def norm_backward(grad_normed, values, gain_row):
    inv_rms = rms_scale(values)
    weighted = grad_normed * gain_row
    grad_gain = jnp.sum(grad_normed * values * inv_rms, axis=0)
    grad_values = inv_rms * weighted - values * inv_rms**3 * jnp.mean(
        weighted * values, axis=-1, keepdims=True
    )
    return (grad_values, grad_gain)


def bucket_onehot():
    places = jnp.arange(SLOT, dtype=jnp.int32)
    offset = places[None, :] - places[:, None]
    distance = jnp.abs(offset)
    bucket = jnp.zeros_like(distance)
    for threshold in bucket_edges:
        bucket = bucket + (distance >= threshold).astype(jnp.int32)
    bucket = bucket + BUCKETS // 2 * (offset > 0).astype(jnp.int32)
    return (bucket[:, :, None] == jnp.arange(BUCKETS, dtype=jnp.int32)).astype(bf16)


def same_sequence(lengths):
    bounds = jnp.cumsum(lengths, axis=-1)
    places = jnp.arange(SLOT, dtype=jnp.int32)
    owners = jnp.sum((places[:, None] >= bounds[:, None, :]).astype(jnp.int32), axis=-1)
    return owners[:, :, None] == owners[:, None, :]


def expert_places(route_ids, experts, capacity):
    blocks = route_ids.shape[0]
    names = jnp.arange(experts, dtype=jnp.int32)
    choose = (route_ids[:, :, None] == names).astype(jnp.int32)
    places = jnp.arange(SLOT, dtype=jnp.int32)
    earlier = (places[:, None] > places[None, :]).astype(bf16)
    before = jnp.einsum(
        "tu,bue->bte", earlier, choose.astype(bf16), preferred_element_type=f32
    ).astype(jnp.int32)
    rank_ids = jnp.sum(before * choose, axis=-1)
    block_ids = jnp.arange(blocks, dtype=jnp.int32)[:, None]
    targets = ((route_ids * blocks + block_ids) * capacity + rank_ids).reshape(-1)
    slots = jnp.arange(experts * blocks * capacity, dtype=jnp.int32)
    placing = (targets[:, None] == slots[None, :]).astype(bf16)
    return (choose.astype(f32).reshape(-1, experts), placing)


def to_experts(row_data, placing):
    packed = jnp.einsum("ts,td->sd", placing, row_data, preferred_element_type=f32).astype(bf16)
    experts = lax.axis_size("dp") // 2
    arrived = chip_all_to_all(packed.reshape(experts, -1, D)).reshape(-1, D)
    return (arrived, pair_swap(arrived))


def from_experts(own, other, placing):
    summed = (own + pair_swap(other.astype(bf16)).astype(f32)).astype(bf16)
    experts = lax.axis_size("dp") // 2
    returned = chip_all_to_all(summed.reshape(experts, -1, D)).reshape(-1, D)
    return dot(placing, returned)


def split_heads(rows):
    return rows.reshape(-1, SLOT, HEADS, HEAD_DIM)


def score_block(queries, keys, relative, same_seq):
    scores = (
        jnp.einsum("bqhd,bkhd->bhqk", queries, keys, preferred_element_type=f32)
        * HEAD_DIM ** (-0.5)
        + relative
    )
    return jnp.where(same_seq[:, None], scores, masked_score)


def gelu_parts(hidden):
    rate, cubic = 0.7978845608028654, 0.044715
    squared = hidden * hidden
    bend = jnp.tanh(rate * hidden * (1.0 + cubic * squared))
    active = 0.5 * hidden * (1.0 + bend)
    slope = 0.5 * (1.0 + bend) + 0.5 * hidden * (1.0 - bend * bend) * rate * (
        1.0 + 3.0 * cubic * squared
    )
    return (active.astype(bf16), slope.astype(bf16))


def layer_forward(inputs, dense, fixed, experts_held):
    gain_rows, qkv_w, out_w, router_w = dense
    relative, same_seq, choose, placing = fixed
    weight_in, weight_out = experts_held
    normed = (inputs * rms_scale(inputs) * gain_rows[0]).astype(bf16)
    projected = dot(normed, qkv_w).astype(bf16)
    queries, keys, values = [split_heads(part) for part in jnp.split(projected, 3, axis=-1)]
    scores = score_block(queries, keys, relative, same_seq)
    top_score = jnp.max(scores, axis=-1, keepdims=True)
    raised = jnp.exp(scores - top_score)
    probs = raised / jnp.sum(raised, axis=-1, keepdims=True)
    weights = probs.astype(bf16)
    attended = (
        jnp.einsum("bhqk,bkhd->bqhd", weights, values, preferred_element_type=f32)
        .astype(bf16)
        .reshape(-1, D)
    )
    middle = inputs + dot(attended, out_w)
    routed = (middle * rms_scale(middle) * gain_rows[1]).astype(bf16)
    route_probs = jax.nn.softmax(dot(routed, router_w), axis=-1)
    gate_prob = jnp.sum(route_probs * choose, axis=-1)
    arrived = to_experts(routed, placing)
    active, slope = zip(*[gelu_parts(dot(rows, weight_in)) for rows in arrived])
    replies = [dot(rows, weight_out) for rows in active]
    result = from_experts(replies[0], replies[1], placing)
    outputs = middle + gate_prob[:, None] * result
    kept = (
        inputs,
        normed,
        (queries, keys, values),
        probs,
        attended,
        middle,
        routed,
        route_probs,
        gate_prob,
        result,
        arrived,
        active,
        slope,
    )
    return (outputs, kept)


def layer_backward(grad_out, kept, dense, fixed, onehot, experts_held):
    (
        inputs,
        normed,
        (queries, keys, values),
        probs,
        attended,
        middle,
        routed,
        route_probs,
        gate_prob,
        result,
        arrived,
        active,
        slope,
    ) = kept
    gain_rows, qkv_w, out_w, router_w = dense
    relative, same_seq, choose, placing = fixed
    weight_in, weight_out = experts_held
    grad_gate = jnp.sum(grad_out * result, axis=-1)
    grad_result = (gate_prob[:, None] * grad_out).astype(bf16)
    grad_rows = to_experts(grad_result, placing)
    grad_hidden = [
        (
            jnp.einsum("rd,fd->rf", rows, weight_out, preferred_element_type=f32)
            * steep.astype(f32)
        ).astype(bf16)
        for rows, steep in zip(grad_rows, slope)
    ]
    grad_sent = [
        jnp.einsum("rf,df->rd", rows, weight_in, preferred_element_type=f32)
        for rows in grad_hidden
    ]
    grad_routed = from_experts(grad_sent[0], grad_sent[1], placing)
    grad_expert_out = jnp.einsum(
        "krf,krd->fd", jnp.stack(active), jnp.stack(grad_rows), preferred_element_type=f32
    )
    grad_expert_in = jnp.einsum(
        "krd,krf->df", jnp.stack(arrived), jnp.stack(grad_hidden), preferred_element_type=f32
    )
    grad_logits = ((grad_gate * gate_prob)[:, None] * (choose - route_probs)).astype(bf16)
    grad_router = jnp.einsum("td,te->de", routed, grad_logits, preferred_element_type=f32)
    grad_routed = grad_routed + jnp.einsum(
        "te,de->td", grad_logits, router_w, preferred_element_type=f32
    )
    grad_middle_norm, grad_gain_two = norm_backward(grad_routed, middle, gain_rows[1])
    grad_middle = grad_out + grad_middle_norm
    grad_branch = grad_middle.astype(bf16)
    grad_out_w = jnp.einsum("tf,td->fd", attended, grad_branch, preferred_element_type=f32)
    grad_attended = split_heads(
        jnp.einsum("td,fd->tf", grad_branch, out_w, preferred_element_type=f32).astype(bf16)
    )
    grad_values = jnp.einsum(
        "bhqk,bqhd->bkhd", probs.astype(bf16), grad_attended, preferred_element_type=f32
    )
    grad_probs = jnp.einsum(
        "bqhd,bkhd->bhqk", grad_attended, values, preferred_element_type=f32
    )
    grad_scores = (
        probs * (grad_probs - jnp.sum(probs * grad_probs, axis=-1, keepdims=True))
    ).astype(bf16)
    scale_qk = HEAD_DIM ** (-0.5)
    grad_queries = (
        jnp.einsum("bhqk,bkhd->bqhd", grad_scores, keys, preferred_element_type=f32) * scale_qk
    )
    grad_keys = (
        jnp.einsum("bhqk,bqhd->bkhd", grad_scores, queries, preferred_element_type=f32) * scale_qk
    )
    grad_table = jnp.einsum(
        "bhqk,qkn->nh", grad_scores, onehot, preferred_element_type=f32
    ).reshape(-1)
    grad_projected = jnp.concatenate(
        [part.astype(bf16).reshape(-1, D) for part in (grad_queries, grad_keys, grad_values)],
        axis=-1,
    )
    grad_qkv = jnp.einsum("td,tf->df", normed, grad_projected, preferred_element_type=f32)
    grad_normed = jnp.einsum("tf,df->td", grad_projected, qkv_w, preferred_element_type=f32)
    grad_inputs_norm, grad_gain_one = norm_backward(grad_normed, inputs, gain_rows[0])
    grad_inputs = grad_middle + grad_inputs_norm
    dense_grads = (
        jnp.stack([grad_gain_one, grad_gain_two]),
        grad_qkv,
        grad_out_w,
        grad_router,
        grad_table,
    )
    return (grad_inputs, dense_grads, (grad_expert_in, grad_expert_out))


def pack_dense(gains, qkv, out, router, table, owners, kind):
    extent = qkv.shape[0] // owners
    entries = jnp.pad(
        table.reshape(owners, -1), ((0, 0), (0, extent - table.size // owners))
    ).reshape(-1, 1)
    extra = jnp.concatenate(
        [router.astype(kind), gains.T.astype(kind), entries.astype(kind)], axis=1
    )
    extra = jnp.pad(extra, ((0, 0), (0, 128 - extra.shape[1])))
    return jnp.concatenate([qkv.astype(kind), out.astype(kind), extra], axis=1)


def unpack_dense(packed, owners, experts):
    qkv, out, extra = packed[:, : 3 * D], packed[:, 3 * D : 4 * D], packed[:, 4 * D :]
    used = packed.shape[0] // owners * BUCKETS * HEADS // D
    table = extra[:, experts + 2].reshape(owners, -1)[:, :used].reshape(-1)
    return (extra[:, experts : experts + 2].T, qkv, out, extra[:, :experts], table)


def scatter_dense(packed):
    devices = lax.axis_size("dp")
    core = lax.axis_index("dp") % 2
    packed = packed.reshape(devices // 2, 2, D // devices, -1)
    mine = lax.dynamic_index_in_dim(packed, core, axis=1, keepdims=False)
    others = lax.dynamic_index_in_dim(packed, 1 - core, axis=1, keepdims=False)
    summed = (mine + pair_swap(others.astype(bf16)).astype(f32)).astype(bf16)
    return jnp.sum(chip_all_to_all(summed).astype(f32), axis=0)


def shards(
    edge_rows,
    lengths,
    routes,
    norm_gains,
    qkv_weight,
    out_weight,
    router_weight,
    bias_table,
    expert_in,
    expert_out,
):
    devices = lax.axis_size("dp")
    experts = devices // 2
    first_section = lax.axis_index("section") == 0
    local_rows = edge_rows[0].astype(f32)
    onehot = bucket_onehot()
    experts_held = (expert_in[0], expert_out[0])
    packed = pack_dense(
        norm_gains[0], qkv_weight[0], out_weight[0], router_weight[0], bias_table[0], 1, bf16
    )
    gathered = lax.all_gather(packed, "dp", axis=0, tiled=True)
    gains, qkv_w, out_w, router_w, table = unpack_dense(gathered, devices, experts)
    dense = (gains.astype(f32), qkv_w, out_w, router_w)
    relative = jnp.einsum(
        "qkb,bh->hqk", onehot, table.reshape(BUCKETS, HEADS), preferred_element_type=f32
    )
    route_ids = routes[0, :, 0].reshape(-1, SLOT)
    choose, placing = expert_places(route_ids, experts, 4 * SLOT // devices)
    fixed = (relative, same_sequence(lengths), choose, placing)
    outputs, _ = layer_forward(local_rows, dense, fixed, experts_held)
    carried = section_shift(outputs.astype(bf16), 1).astype(f32)
    inputs = jnp.where(first_section, local_rows, carried)
    outputs, kept = layer_forward(inputs, dense, fixed, experts_held)
    grad_inputs, _, _ = layer_backward(local_rows, kept, dense, fixed, onehot, experts_held)
    carried = section_shift(grad_inputs.astype(bf16), -1).astype(f32)
    grad_out = jnp.where(first_section, carried, local_rows)
    grad_inputs, dense_grads, expert_grads = layer_backward(
        grad_out, kept, dense, fixed, onehot, experts_held
    )
    edge_results = jnp.where(first_section, grad_inputs, outputs)
    total = scatter_dense(pack_dense(*dense_grads, devices, f32))
    grad_gains, grad_qkv, grad_out_w, grad_router, grad_table = unpack_dense(total, 1, experts)
    return (
        edge_results[None],
        grad_gains[None],
        grad_qkv[None],
        grad_out_w[None],
        grad_router[None],
        grad_table[None],
        expert_grads[0][None],
        expert_grads[1][None],
    )


def solution(mesh):
    return jax.shard_map(
        shards,
        mesh=mesh,
        in_specs=(
            P("section", "dp", None),
            P("dp", None),
            P("section", "dp", None),
            P("section", None, "dp"),
            P("section", "dp", None),
            P("section", "dp", None),
            P("section", "dp", None),
            P("section", "dp"),
            P("section", None, "dp"),
            P("section", "dp", None),
        ),
        out_specs=(
            P("section", "dp", None),
            P("section", None, "dp"),
            P("section", "dp", None),
            P("section", "dp", None),
            P("section", "dp", None),
            P("section", "dp"),
            P("section", None, "dp"),
            P("section", "dp", None),
        ),
        check_vma=False,
    )
```

time: 848 us -> 558 us (0.66)
  blocking collectives: 188 us -> 71.8 us
  waiting for transfers between devices: 255 us -> 186 us
  other arithmetic: 82.3 us -> 32.8 us
  starting transfers between devices: 57.6 us -> 32.9 us
  matrix products: 152 us -> 134 us
    reduce_scatter x2 -> x0, waiting for transfers between devices: 159 us -> none  [the longest x1 94 us: shards(): lax.psum_scatter(dense_total[1], 'dp', scatter_dimension=0, tiled=True)]
    unnamed x2 -> x0, blocking collectives: 68.8 us -> none
    all_gather x2 -> x0, blocking collectives: 45.4 us -> none  [the longest x1 26.5 us: shards(): lax.all_gather(local_dense[3], 'dp', axis=0, tiled=True)]
    all_gather x2 -> x1, waiting for transfers between devices: 8.12 us -> 51 us  [shards(): gathered = lax.all_gather(packed, 'dp', axis=0, tiled=True)]
    all_to_all x9 -> x6, waiting for transfers between devices: 66.7 us -> 104 us  [chip_all_to_all(): lax.all_to_all(block, 'dp', split_axis=0, concat_axis=0, tiled=True, axis...]
    all_to_all x9 -> x6, starting transfers between devices: 46.7 us -> 26.5 us  [chip_all_to_all(): lax.all_to_all(block, 'dp', split_axis=0, concat_axis=0, tiled=True, axis...]
    dot_general x76 -> x52, matrix products: 152 us -> 134 us  [the longest x16 47.7 us: dot(): return jnp.dot(lhs, rhs, preferred_element_type=f32)]
    gather x6 -> x0, local copies, waits for them, and re-layouts: 17.9 us -> none  [gather_slots(): return jnp.take(summed, targets, axis=0)]
  transfers between devices with their start and end apart: 19 -> 18, of which waited for: 15 -> 13; matrix products, arithmetic and copies ran while one was open for 24% -> 14% of each run, Pallas kernels for 0% -> 0%
where the time goes in v1:
time: 558 us; the launch traced here: 549 us
  waiting for transfers between devices  186 us (33%)
  matrix products  134 us (24%)
  local copies, waits for them, and re-layouts  75.7 us (14%)
  blocking collectives  71.8 us (13%)
  starting transfers between devices  32.9 us (6%)
  other arithmetic  32.8 us (6%)
  between operations  15.7 us (3%)
    all_to_all x6, waiting for transfers between devices, chip_all_to_all(): lax.all_to_all(block, 'dp', split_axis=0, concat_axis=0, tiled=True, axis...  104 us
    all_to_all x3, blocking collectives, chip_all_to_all(): lax.all_to_all(block, 'dp', split_axis=0, concat_axis=0, tiled=True, axis...  71.8 us
    all_gather x1, waiting for transfers between devices, shards(): gathered = lax.all_gather(packed, 'dp', axis=0, tiled=True)  51 us
    dot_general x16, matrix products, dot(): return jnp.dot(lhs, rhs, preferred_element_type=f32)  47.7 us
    all_to_all x6, starting transfers between devices, chip_all_to_all(): lax.all_to_all(block, 'dp', split_axis=0, concat_axis=0, tiled=True, axis...  26.5 us
    ppermute x2, waiting for transfers between devices, section_shift(): return lax.ppermute(block, 'section', route)  18.5 us
    dot_general x4, matrix products, layer_backward(): jnp.einsum('rf,df->rd', rows, weight_in, preferred_element_type=f32)  18.1 us
    unnamed x177, local copies, waits for them, and re-layouts  15.6 us
  transfers between devices with their start and end apart: 18, of which 13 were waited for; matrix products, arithmetic and copies ran while one was open for 14% of the time, Pallas kernels for 0%

profile of v1, /device:TPU:0, one launch (start us, length us, event | category | flops | bytes accessed | tf_op | source)
XLA Modules:
  0.0 548.8 jit_solution(10258697293099966708)
XLA Ops:
  12.0 3.2 copy.221
  16.9 51.0 %all-gather.2.cloned.1.call-done = bf16[768,3200]{1,0:T(8,128)(2,1)} async-done(((bf16[48,3200]{1,0:T(8,128)(2,1)}), bf16[768,3200]{1,0:T(8,128)(2,1)}) %all-gather.2.cloned.1.call-update) | async-done | bytes 4915216 | tf_op jit(solution)/shard_map/all_gather | solution.py:312
  74.7 3.4 convolution_convert_fusion.1
  93.5 2.6 fusion.88
  99.0 23.7 %all_to_all.45 = bf16[8,64,768]{2,1,0:T(8,128)(2,1)S(1)} all-to-all(bf16[8,64,768]{2,1,0:T(8,128)(2,1)S(1)} %bitcast.311), channel_id=1, replica_groups={{0,2,4,6,8,10,12,14},{1,3,5,7,9,11,13,15},{16,18,20,22,24,26,28,30},{17..., dimensions={0} | all-to-all | bytes 1572864 | tf_op jit(solution)/shard_map/all_to_all | solution.py:37
  126.0 5.6 %fusion.68 = bf16[512,768]{1,0:T(8,128)(2,1)} fusion(bf16[1,1536,768]{2,1,0:T(8,128)(2,1)S(1)} %copy-done, bf16[512,768]{1,0:T(8,128)(2,1)} %collective-permute-done, bf16[1,768,1536]{2,1,0:T(8,128)(2,1)} %param.18), kind=kOutput, calls=%fused_computation.102 | convolution fusion | flops 2423390208 | bytes 6291456 | tf_op jit(solution)/shard_map/dot_general | solution.py:21
  131.7 2.5 collective-permute-done.1
  134.2 5.8 %add_convert_fusion.5 = bf16[512,768]{1,0:T(8,128)(2,1)} fusion(bf16[512,768]{1,0:T(8,128)(2,1)} %collective-permute-done.1, bf16[1,1536,768]{2,1,0:T(8,128)(2,1)S(1)} %copy-done, bf16[512,768]{1,0:T(8,128)(2,1)} %bitcast.330, bf16[1,768,1536]{2,1,0:T(8,128)(2,1)} %param.18), kind=kOutput, calls=%fused_computation.95 | convolution fusion | flops 2424176640 | bytes 7077888 | tf_op jit(solution)/shard_map/dot_general | solution.py:21
  139.9 4.2 all-to-all-start.1
  146.1 18.8 %all-to-all-done.1 = bf16[8,64,768]{2,1,0:T(8,128)(2,1)} async-done(((bf16[8,64,768]{2,1,0:T(8,128)(2,1)}), bf16[8,64,768]{2,1,0:T(8,128)(2,1)}, u32[]{:S(2)}, u32[]{:S(2)}) %all-to-all-start.1) | async-done | bytes 786464 | tf_op jit(solution)/shard_map/all_to_all | solution.py:37
  167.2 3.4 collective-permute-start.2
  170.6 8.1 %collective-permute-done.2 = bf16[256,768]{1,0:T(8,128)(2,1)S(1)} collective-permute-done((bf16[256,768]{1,0:T(8,128)(2,1)}, bf16[256,768]{1,0:T(8,128)(2,1)S(1)}, u32[]{:S(2)}, u32[]{:S(2)}) %collective-permute-start.2) | collective-permute-done | bytes 393248 | tf_op jit(solution)/shard_map/ppermute | solution.py:27
  179.5 3.2 convolution_convert_fusion
  207.0 23.8 %all_to_all.46 = bf16[8,64,768]{2,1,0:T(8,128)(2,1)} all-to-all(bf16[8,64,768]{2,1,0:T(8,128)(2,1)S(1)} %bitcast.313), channel_id=1, replica_groups={{0,2,4,6,8,10,12,14},{1,3,5,7,9,11,13,15},{16,18,20,22,24,26,28,30},{17..., dimensions={0} | all-to-all | bytes 1572864 | tf_op jit(solution)/shard_map/all_to_all | solution.py:37
  239.0 4.6 all-to-all-start.2
  243.6 3.3 fusion.32
  247.0 2.8 fusion.71
  250.3 14.4 %all-to-all-done.2 = bf16[8,64,768]{2,1,0:T(8,128)(2,1)} async-done(((bf16[8,64,768]{2,1,0:T(8,128)(2,1)}), bf16[8,64,768]{2,1,0:T(8,128)(2,1)}, u32[]{:S(2)}, u32[]{:S(2)}) %all-to-all-start.2) | async-done | bytes 786464 | tf_op jit(solution)/shard_map/all_to_all | solution.py:37
  264.7 3.3 fusion.36
  268.0 4.6 add_convert_fusion.3
  272.6 4.2 all-to-all-start.5
  276.8 7.0 %fusion.62 = bf16[512,768]{1,0:T(8,128)(2,1)} fusion(bf16[1,768,1536]{2,1,0:T(8,128)(2,1)} %param.18, bf16[512,768]{1,0:T(8,128)(2,1)} %collective-permute-done.3, bf16[1,1536,768]{2,1,0:T(8,128)(2,1)S(1)} %copy-done, f32[512,1536]{1,0:T(8,128)} %copy-done.5), kind=kOutput, calls=%fused_computation.100 | convolution fusion | flops 2432040960 | bytes 9437184 | tf_op jit(solution)/shard_map/rf,df->rd/dot_general | solution.py:203
  284.3 7.4 %fusion.34 = f32[512,768]{1,0:T(8,128)} fusion(bf16[1,768,1536]{2,1,0:T(8,128)(2,1)} %param.18, bf16[512,768]{1,0:T(8,128)(2,1)} %bitcast.25, bf16[1,1536,768]{2,1,0:T(8,128)(2,1)S(1)} %copy-done, f32[512,1536]{1,0:T(8,128)} %copy-done.28), kind=kOutput, calls=%fused_computation.55 | convolution fusion | flops 2431647744 | bytes 10223616 | tf_op jit(solution)/shard_map/rf,df->rd/dot_general | solution.py:203
  291.7 2.7 add_convert_fusion.4
  294.4 3.5 all-to-all-done.5
  297.9 4.4 all-to-all-start.4
  307.6 15.1 %all-to-all-done.4 = bf16[8,64,768]{2,1,0:T(8,128)(2,1)} async-done(((bf16[8,64,768]{2,1,0:T(8,128)(2,1)}), bf16[8,64,768]{2,1,0:T(8,128)(2,1)}, u32[]{:S(2)}, u32[]{:S(2)}) %all-to-all-start.4) | async-done | bytes 786464 | tf_op jit(solution)/shard_map/all_to_all | solution.py:37
  325.5 2.6 convolution_convert_fusion.9
  331.9 3.4 fusion.90
  344.6 10.4 %collective-permute-done.7 = bf16[256,768]{1,0:T(8,128)(2,1)S(1)} collective-permute-done((bf16[256,768]{1,0:T(8,128)(2,1)S(1)}, bf16[256,768]{1,0:T(8,128)(2,1)S(1)}, u32[]{:S(2)}, u32[]{:S(2)}) %collective-permute-start.7) | collective-permute-done | bytes 393248 | tf_op jit(solution)/shard_map/ppermute | solution.py:27
  355.6 24.4 %all_to_all.47 = bf16[8,64,768]{2,1,0:T(8,128)(2,1)S(1)} all-to-all(bf16[8,64,768]{2,1,0:T(8,128)(2,1)S(1)} %bitcast.332), channel_id=1, replica_groups={{0,2,4,6,8,10,12,14},{1,3,5,7,9,11,13,15},{16,18,20,22,24,26,28,30},{17..., dimensions={0} | all-to-all | bytes 1572864 | tf_op jit(solution)/shard_map/all_to_all | solution.py:37
  382.3 2.7 fusion.12
  387.4 2.7 fusion.10
  392.5 4.4 all-to-all-start.7
  403.0 14.6 %all-to-all-done.7 = bf16[8,64,768]{2,1,0:T(8,128)(2,1)} async-done(((bf16[8,64,768]{2,1,0:T(8,128)(2,1)}), bf16[8,64,768]{2,1,0:T(8,128)(2,1)}, u32[]{:S(2)}, u32[]{:S(2)}) %all-to-all-start.7) | async-done | bytes 786464 | tf_op jit(solution)/shard_map/all_to_all | solution.py:37
  417.6 2.6 multiply_reduce_fusion.2
  422.1 2.5 convolution_convert_fusion.7
  428.4 3.4 fusion.91
  448.3 5.1 multiply_reduce_fusion.3
  455.8 2.8 fusion.227
  459.3 3.7 copy-done.2
  464.7 5.0 collective-permute-done.10
  469.8 5.0 fusion.2
  474.8 4.6 all-to-all-start.8
  481.7 3.0 fusion.228
  486.9 5.5 %convolution_bitcast_fusion.1 = f32[1,768,1536]{2,1,0:T(8,128)} fusion(bf16[1,512,1536]{2,1,0:T(8,128)(2,1)S(1)} %bitcast.350, bf16[1,512,1536]{2,1,0:T(8,128)(2,1)S(1)} %bitcast.351, bf16[1,512,768]{1,2,0:T(8,128)(2,1)} %bitcast.54, bf16[1,512,768]{1,2,0:T(8,128)(2,1)S(1)} %copy-done.42), kind=kOutput, calls=%fused_computation.15 | convolution fusion | flops 2418278400 | bytes 9437184 | tf_op jit(solution)/shard_map/krd,krf->df/dot_general | solution.py:210
  492.5 4.4 convolution_bitcast_fusion
  498.2 37.7 %all-to-all-done.8 = bf16[8,48,3200]{2,1,0:T(8,128)(2,1)} async-done(((bf16[8,48,3200]{2,1,0:T(8,128)(2,1)}), bf16[8,48,3200]{2,1,0:T(8,128)(2,1)}, u32[]{:S(2)}, u32[]{:S(2)}) %all-to-all-start.8) | async-done | bytes 2457632 | tf_op jit(solution)/shard_map/all_to_all | solution.py:37
  (315 shorter events, 145.9 us)
Async XLA Ops:
  7.2 118.8 %copy-start = (bf16[1,1536,768]{2,1,0:T(8,128)(2,1)S(1)}, bf16[1,1536,768]{2,1,0:T(8,128)(2,1)}, u32[]{:S(2)}) copy-start(bf16[1,1536,768]{2,1,0:T(8,128)(2,1)} %param.19) | copy-start | bytes 7077892
  7.2 8.0 %copy-start.56 = (s32[1,256,1]{1,2,0:T(1,128)S(1)}, s32[1,256,1]{1,2,0:T(1,128)}, u32[]{:S(2)}) copy-start(s32[1,256,1]{1,2,0:T(1,128)} %param.12) | copy-start | bytes 3076
  7.2 8.3 %copy-start.1 = (bf16[1,256,768]{2,1,0:T(8,128)(2,1)S(1)}, bf16[1,256,768]{2,1,0:T(8,128)(2,1)}, u32[]{:S(2)}) copy-start(bf16[1,256,768]{2,1,0:T(8,128)(2,1)} %param.10) | copy-start | bytes 1179652
  7.2 60.8 %all-gather.2.cloned.1.call-start = ((), (), s32[]{:S(2)}) async-start(), calls=%async_computation.9 | async-start | bytes 5222400 | tf_op jit(solution)/shard_map/all_gather | solution.py:312
  11.7 59.1 %copy-start.46 = (s32[128,128]{0,1:T(8,128)}, s32[128,128]{0,1:T(8,128)S(1)}, u32[]{:S(2)}) copy-start(s32[128,128]{0,1:T(8,128)S(1)} %select_add_fusion) | copy-start | bytes 196612
  16.2 189.5 %copy-start.53 = (s32[256]{0:T(256)}, s32[256]{0:T(256)S(1)}, u32[]{:S(2)}) copy-start(s32[256]{0:T(256)S(1)} %bitcast_add_fusion.1) | copy-start | bytes 3076
  70.8 270.4 %copy-start.50 = (f32[768]{0:T(1024)}, f32[768]{0:T(1024)S(1)}, u32[]{:S(2)}) copy-start(f32[768]{0:T(1024)S(1)} %get-tuple-element.45) | copy-start | bytes 9220
  74.7 15.8 %copy-start.17 = (f32[12,128,128]{1,2,0:T(8,128)}, f32[12,128,128]{1,2,0:T(8,128)S(1)}, u32[]{:S(2)}) copy-start(f32[12,128,128]{1,2,0:T(8,128)S(1)} %copy.222) | copy-start | bytes 2359300
  98.4 25.2 %copy-start.72 = (f32[256]{0:T(256)}, f32[256]{0:T(256)S(1)}, u32[]{:S(2)}) copy-start(f32[256]{0:T(256)S(1)} %add_rsqrt_fusion.2) | copy-start | bytes 3076
  123.5 2.4 collective-permute-start
  131.6 2.6 collective-permute-start.1
  139.9 24.9 %all-to-all-start.1 = ((bf16[8,64,768]{2,1,0:T(8,128)(2,1)}), bf16[8,64,768]{2,1,0:T(8,128)(2,1)}, u32[]{:S(2)}, u32[]{:S(2)}) async-start(bf16[8,64,768]{2,1,0:T(8,128)(2,1)} %bitcast.331), calls=%async_computation.1 | async-start | bytes 1572864 | tf_op jit(solution)/shard_map/all_to_all | solution.py:37
  167.2 11.5 %collective-permute-start.2 = (bf16[256,768]{1,0:T(8,128)(2,1)}, bf16[256,768]{1,0:T(8,128)(2,1)S(1)}, u32[]{:S(2)}, u32[]{:S(2)}) collective-permute-start(bf16[256,768]{1,0:T(8,128)(2,1)} %fusion.83), channel_id=1, source_target_pairs={{0,16},{1,17},{2,18},{3,19},{4,20},{5,21},{6,22},{7,23},{8,24},{9,... | collective-permute-start | bytes 1179656 | tf_op jit(solution)/shard_map/ppermute | solution.py:27
  183.7 11.4 %copy-start.18 = (f32[12,128,128]{1,2,0:T(8,128)S(1)}, f32[12,128,128]{1,2,0:T(8,128)}, u32[]{:S(2)}) copy-start(f32[12,128,128]{1,2,0:T(8,128)} %copy-done.17) | copy-start | bytes 2359300
  205.6 27.5 %copy-start.57 = (f32[256]{0:T(256)}, f32[256]{0:T(256)S(1)}, u32[]{:S(2)}) copy-start(f32[256]{0:T(256)S(1)} %get-tuple-element.57) | copy-start | bytes 3076
  233.1 10.5 %collective-permute-start.4 = (bf16[512,768]{0,1:T(8,128)(2,1)}, bf16[512,768]{0,1:T(8,128)(2,1)}, u32[]{:S(2)}, u32[]{:S(2)}) collective-permute-start(bf16[512,768]{0,1:T(8,128)(2,1)} %copy.234), channel_id=1, source_target_pairs={{0,1},{1,0},{2,3},{3,2},{4,5},{5,4},{6,7},{7,6},{8,9},{9,8},{10,11... | collective-permute-start | bytes 2359304 | tf_op jit(solution)/shard_map/ppermute | solution.py:31
  239.0 25.7 %all-to-all-start.2 = ((bf16[8,64,768]{2,1,0:T(8,128)(2,1)}), bf16[8,64,768]{2,1,0:T(8,128)(2,1)}, u32[]{:S(2)}, u32[]{:S(2)}) async-start(bf16[8,64,768]{2,1,0:T(8,128)(2,1)} %bitcast.310), calls=%async_computation.2 | async-start | bytes 1572864 | tf_op jit(solution)/shard_map/all_to_all | solution.py:37
  249.8 18.2 %collective-permute-start.6 = (bf16[512,768]{1,0:T(8,128)(2,1)}, bf16[512,768]{1,0:T(8,128)(2,1)}, u32[]{:S(2)}, u32[]{:S(2)}) collective-permute-start(bf16[512,768]{1,0:T(8,128)(2,1)} %fusion.71), channel_id=1, source_target_pairs={{0,1},{1,0},{2,3},{3,2},{4,5},{5,4},{6,7},{7,6},{8,9},{9,8},{10,11... | collective-permute-start | bytes 2359304 | tf_op jit(solution)/shard_map/ppermute | solution.py:31
  264.7 12.1 %collective-permute-start.3 = (bf16[512,768]{1,0:T(8,128)(2,1)}, bf16[512,768]{1,0:T(8,128)(2,1)}, u32[]{:S(2)}, u32[]{:S(2)}) collective-permute-start(bf16[512,768]{1,0:T(8,128)(2,1)} %bitcast.25), channel_id=1, source_target_pairs={{0,1},{1,0},{2,3},{3,2},{4,5},{5,4},{6,7},{7,6},{8,9},{9,8},{10,11... | collective-permute-start | bytes 2359304 | tf_op jit(solution)/shard_map/ppermute | solution.py:31
  268.0 4.6 copy-start.28
  272.6 25.3 %all-to-all-start.5 = ((bf16[8,64,768]{2,1,0:T(8,128)(2,1)}), bf16[8,64,768]{2,1,0:T(8,128)(2,1)}, u32[]{:S(2)}, u32[]{:S(2)}) async-start(bf16[8,64,768]{2,1,0:T(8,128)(2,1)} %bitcast.328), calls=%async_computation.5 | async-start | bytes 1572864 | tf_op jit(solution)/shard_map/all_to_all | solution.py:37
  283.8 7.9 %collective-permute-start.5 = (bf16[512,768]{1,0:T(8,128)(2,1)}, bf16[512,768]{1,0:T(8,128)(2,1)}, u32[]{:S(2)}, u32[]{:S(2)}) collective-permute-start(bf16[512,768]{1,0:T(8,128)(2,1)} %fusion.62), channel_id=1, source_target_pairs={{0,1},{1,0},{2,3},{3,2},{4,5},{5,4},{6,7},{7,6},{8,9},{9,8},{10,11... | collective-permute-start | bytes 2359304 | tf_op jit(solution)/shard_map/ppermute | solution.py:31
  297.9 24.7 %all-to-all-start.4 = ((bf16[8,64,768]{2,1,0:T(8,128)(2,1)}), bf16[8,64,768]{2,1,0:T(8,128)(2,1)}, u32[]{:S(2)}, u32[]{:S(2)}) async-start(bf16[8,64,768]{2,1,0:T(8,128)(2,1)} %bitcast.312), calls=%async_computation.4 | async-start | bytes 1572864 | tf_op jit(solution)/shard_map/all_to_all | solution.py:37
  335.3 5.9 %slice-start = ((s8[4915200]{0:T(1024)(128)(4,1)}), s8[4194304]{0:T(1024)(128)(4,1)S(1)}, s32[]{:S(2)}) async-start(s8[4915200]{0:T(1024)(128)(4,1)} %bitcast.314), calls=%async_computation.10 | async-start | bytes 8388608
  342.6 12.5 %copy-start.54 = (s32[256]{0:T(256)S(1)}, s32[256]{0:T(256)}, u32[]{:S(2)}) copy-start(s32[256]{0:T(256)} %copy-done.53) | copy-start | bytes 3076
  342.6 12.4 %copy-start.61 = (f32[256]{0:T(256)S(1)}, f32[256]{0:T(256)}, u32[]{:S(2)}) copy-start(f32[256]{0:T(256)} %copy-done.60) | copy-start | bytes 3076
  343.1 39.2 %copy-start.6 = (f32[512,1536]{1,0:T(8,128)S(1)}, f32[512,1536]{1,0:T(8,128)}, u32[]{:S(2)}) copy-start(f32[512,1536]{1,0:T(8,128)} %copy-done.5) | copy-start | bytes 9437188
  343.1 11.9 %collective-permute-start.7 = (bf16[256,768]{1,0:T(8,128)(2,1)S(1)}, bf16[256,768]{1,0:T(8,128)(2,1)S(1)}, u32[]{:S(2)}, u32[]{:S(2)}) collective-permute-start(bf16[256,768]{1,0:T(8,128)(2,1)S(1)} %add_convert_fusion.6), channel_id=1, source_target_pairs={{16,0},{17,1},{18,2},{19,3},{20,4},{21,5},{22,6},{23,7},{24,8},{25... | collective-permute-start | bytes 1179656 | tf_op jit(solution)/shard_map/ppermute | solution.py:27
  355.0 25.0 %copy-start.35 = (bf16[256,768]{1,0:T(8,128)(2,1)}, bf16[256,768]{1,0:T(8,128)(2,1)S(1)}, u32[]{:S(2)}) copy-start(bf16[256,768]{1,0:T(8,128)(2,1)S(1)} %collective-permute-done.7) | copy-start | bytes 1179652
  380.0 6.7 %copy-start.39 = (bf16[8,64,768]{2,1,0:T(8,128)(2,1)}, bf16[8,64,768]{2,1,0:T(8,128)(2,1)S(1)}, u32[]{:S(2)}) copy-start(bf16[8,64,768]{2,1,0:T(8,128)(2,1)S(1)} %all_to_all.47) | copy-start | bytes 2359300
  380.0 5.0 copy-start.30
  380.0 2.3 collective-permute-start.8
  386.4 3.7 collective-permute-start.9
  392.5 25.2 %all-to-all-start.7 = ((bf16[8,64,768]{2,1,0:T(8,128)(2,1)}), bf16[8,64,768]{2,1,0:T(8,128)(2,1)}, u32[]{:S(2)}, u32[]{:S(2)}) async-start(bf16[8,64,768]{2,1,0:T(8,128)(2,1)} %bitcast.327), calls=%async_computation.7 | async-start | bytes 1572864 | tf_op jit(solution)/shard_map/all_to_all | solution.py:37
  422.1 6.3 %copy-start.49 = (f32[2,12,128]{2,1,0:T(8,128)S(1)}, f32[2,12,128]{2,1,0:T(8,128)}, u32[]{:S(2)}) copy-start(f32[2,12,128]{2,1,0:T(8,128)} %get-tuple-element.62) | copy-start | bytes 36868
  441.2 7.0 %copy-start.51 = (f32[768]{0:T(1024)S(1)}, f32[768]{0:T(1024)}, u32[]{:S(2)}) copy-start(f32[768]{0:T(1024)} %copy-done.50) | copy-start | bytes 9220
  441.2 7.0 %copy-start.66 = (f32[256]{0:T(256)S(1)}, f32[256]{0:T(256)}, u32[]{:S(2)}) copy-start(f32[256]{0:T(256)} %copy-done.64) | copy-start | bytes 3076
  448.2 5.2 copy-start.31
  448.2 5.1 copy-start.70
  448.3 5.2 copy-start.52
  448.3 5.2 copy-start.71
  464.7 5.0 collective-permute-start.10
  474.8 61.2 %all-to-all-start.8 = ((bf16[8,48,3200]{2,1,0:T(8,128)(2,1)}), bf16[8,48,3200]{2,1,0:T(8,128)(2,1)}, u32[]{:S(2)}, u32[]{:S(2)}) async-start(bf16[8,48,3200]{2,1,0:T(8,128)(2,1)} %fusion.2), calls=%async_computation.8 | async-start | bytes 4915200 | tf_op jit(solution)/shard_map/all_to_all | solution.py:37
  486.9 5.5 %copy-start.40 = (bf16[8,64,768]{2,1,0:T(8,128)(2,1)S(1)}, bf16[8,64,768]{2,1,0:T(8,128)(2,1)}, u32[]{:S(2)}) copy-start(bf16[8,64,768]{2,1,0:T(8,128)(2,1)} %copy-done.39) | copy-start | bytes 2359300
  486.9 5.5 %copy-start.79 = (bf16[512,768]{1,0:T(8,128)(2,1)S(1)}, bf16[512,768]{1,0:T(8,128)(2,1)}, u32[]{:S(2)}) copy-start(bf16[512,768]{1,0:T(8,128)(2,1)} %copy-done.78) | copy-start | bytes 2359300
  492.4 4.5 copy-start.77
  492.4 4.5 copy-start.10
  492.4 4.5 copy-start.15
  (56 other events, 125.4 us)
Sparse Core Ops, SparseCore 0:
  10.8 57.1 all-gather.1

commit v2 on v1

v2 whole, which is shorter than its diff:
```python
import functools

import jax
import jax.numpy as jnp
from jax import lax
from jax.experimental import pallas as pl
from jax.experimental.pallas import tpu as pltpu
from jax.sharding import PartitionSpec as P

D = 768
HEADS = 12
HEAD_DIM = 64
BUCKETS = 32
SLOT = 128


norm_eps = 1e-06
masked_score = -1e30
bucket_edges = (1, 2, 3, 4, 5, 6, 7, 8, 12, 16, 23, 32, 46, 64, 91)
bf16 = jnp.bfloat16
f32 = jnp.float32


def dot(lhs, rhs):
    return jnp.dot(lhs, rhs, preferred_element_type=f32)


def section_shift(block, distance):
    devices = range(lax.axis_size("section"))
    route = [(i - distance, i) for i in devices if i - distance in devices]
    return lax.ppermute(block, "section", route)


def pair_swap(block):
    return lax.ppermute(block, "dp", [(i, i ^ 1) for i in range(lax.axis_size("dp"))])


def chip_all_to_all(block):
    devices = lax.axis_size("dp")
    groups = [list(range(core, devices, 2)) for core in range(2)]
    return lax.all_to_all(
        block, "dp", split_axis=0, concat_axis=0, tiled=True, axis_index_groups=groups
    )


def rms_scale(values):
    return lax.rsqrt(jnp.mean(values * values, axis=-1, keepdims=True) + norm_eps)


def norm_backward(grad_normed, values, gain_row):
    inv_rms = rms_scale(values)
    weighted = grad_normed * gain_row
    grad_gain = jnp.sum(grad_normed * values * inv_rms, axis=0)
    grad_values = inv_rms * weighted - values * inv_rms**3 * jnp.mean(
        weighted * values, axis=-1, keepdims=True
    )
    return (grad_values, grad_gain)


def bucket_onehot():
    offset = jnp.arange(2 * SLOT, dtype=jnp.int32) - SLOT
    distance = jnp.abs(offset)
    bucket = jnp.zeros_like(distance)
    for threshold in bucket_edges:
        bucket = bucket + (distance >= threshold).astype(jnp.int32)
    bucket = bucket + BUCKETS // 2 * (offset > 0).astype(jnp.int32)
    return (bucket[:, None] == jnp.arange(BUCKETS, dtype=jnp.int32)).astype(f32)


def same_sequence(lengths):
    bounds = jnp.cumsum(lengths, axis=-1)
    places = jnp.arange(SLOT, dtype=jnp.int32)
    owners = jnp.sum((places[:, None] >= bounds[:, None, :]).astype(jnp.int32), axis=-1)
    return (owners[:, :, None] == owners[:, None, :]).astype(f32)


def expert_places(route_ids, experts, capacity):
    blocks = route_ids.shape[0]
    names = jnp.arange(experts, dtype=jnp.int32)
    choose = (route_ids[:, :, None] == names).astype(jnp.int32)
    places = jnp.arange(SLOT, dtype=jnp.int32)
    earlier = (places[:, None] > places[None, :]).astype(bf16)
    before = jnp.einsum(
        "tu,bue->bte", earlier, choose.astype(bf16), preferred_element_type=f32
    ).astype(jnp.int32)
    rank_ids = jnp.sum(before * choose, axis=-1)
    block_ids = jnp.arange(blocks, dtype=jnp.int32)[:, None]
    targets = ((route_ids * blocks + block_ids) * capacity + rank_ids).reshape(-1)
    slots = jnp.arange(experts * blocks * capacity, dtype=jnp.int32)
    placing = (targets[:, None] == slots[None, :]).astype(bf16)
    return (targets, placing)


def to_experts(packed):
    experts = lax.axis_size("dp") // 2
    arrived = chip_all_to_all(packed.reshape(experts, -1, D)).reshape(-1, D)
    return (arrived, pair_swap(arrived))


def from_experts(own, other):
    summed = (own + pair_swap(other.astype(bf16)).astype(f32)).astype(bf16)
    experts = lax.axis_size("dp") // 2
    return chip_all_to_all(summed.reshape(experts, -1, D)).reshape(-1, D)


def dot_nt(lhs, rhs):
    return lax.dot_general(lhs, rhs, (((1,), (1,)), ((), ())), preferred_element_type=f32)


def dot_tn(lhs, rhs):
    return lax.dot_general(lhs, rhs, (((0,), (0,)), ((), ())), preferred_element_type=f32)


def lane_masks():
    low = lax.broadcasted_iota(jnp.int32, (1, 2 * HEAD_DIM), 1) < HEAD_DIM
    first = jnp.where(low, 1.0, 0.0)
    return (low, first.astype(bf16), (1.0 - first).astype(bf16))


def both_heads(slab, first, second):
    return jnp.concatenate([slab * first, slab * second], axis=0)


def own_lanes(low, stacked):
    return jnp.where(low, stacked[:SLOT], stacked[SLOT:])


def front_kernel(
    experts,
    inputs_ref,
    gains_ref,
    weight_ref,
    router_ref,
    diagonals_ref,
    same_ref,
    route_ref,
    target_ref,
    packed_ref,
    projected_ref,
    probs_ref,
    attended_ref,
    middle_ref,
    route_probs_ref,
    gate_ref,
):
    blocks = inputs_ref.shape[0] // SLOT
    inputs = inputs_ref[...]
    normed = (inputs * rms_scale(inputs) * gains_ref[0:1]).astype(bf16)
    projected_ref[...] = dot(normed, weight_ref[:, : 3 * D]).astype(bf16)
    low, first, second = lane_masks()
    width = 2 * HEAD_DIM
    for pair in range(HEADS // 2):
        relative = jnp.concatenate(
            [
                pltpu.roll(
                    jnp.broadcast_to(diagonals_ref[head : head + 1], (SLOT, 2 * SLOT)),
                    SLOT,
                    1,
                    stride=1,
                    stride_axis=0,
                )[:, :SLOT]
                for head in (2 * pair, 2 * pair + 1)
            ],
            axis=0,
        )
        for block in range(blocks):
            rows = slice(block * SLOT, (block + 1) * SLOT)
            queries, keys, values = [
                projected_ref[rows, part * D + pair * width : part * D + (pair + 1) * width]
                for part in range(3)
            ]
            same = same_ref[block]
            scores = (
                dot_nt(both_heads(queries, first, second), keys) * HEAD_DIM ** (-0.5) + relative
            )
            scores = jnp.where(jnp.concatenate([same, same], axis=0) > 0, scores, masked_score)
            raised = jnp.exp(scores - jnp.max(scores, axis=-1, keepdims=True))
            probs = raised / jnp.sum(raised, axis=-1, keepdims=True)
            probs_ref[block, pair] = probs
            attended_ref[rows, pair * width : (pair + 1) * width] = own_lanes(
                low, dot(probs.astype(bf16), values)
            ).astype(bf16)
    middle = inputs + dot(attended_ref[...], weight_ref[:, 3 * D :])
    middle_ref[...] = middle
    routed = (middle * rms_scale(middle) * gains_ref[1:2]).astype(bf16)
    logits = dot_nt(routed, router_ref[...])
    names = lax.broadcasted_iota(jnp.int32, (1, logits.shape[1]), 1)
    logits = jnp.where(names < experts, logits, masked_score)
    raised = jnp.exp(logits - jnp.max(logits, axis=-1, keepdims=True))
    route_probs = raised / jnp.sum(raised, axis=-1, keepdims=True)
    route_probs_ref[...] = route_probs
    gate_ref[...] = jnp.sum(
        jnp.where(names == route_ref[...], route_probs, 0.0), axis=-1, keepdims=True
    )
    slots = lax.broadcasted_iota(jnp.int32, (packed_ref.shape[0], 1), 0)
    placing = jnp.where(slots == target_ref[...], 1.0, 0.0).astype(bf16)
    packed_ref[...] = dot(placing, routed).astype(bf16)


def back_kernel(
    experts,
    full,
    grad_out_ref,
    returned_ref,
    target_ref,
    route_ref,
    inputs_ref,
    gains_ref,
    weight_ref,
    router_ref,
    projected_ref,
    probs_ref,
    attended_ref,
    middle_ref,
    route_probs_ref,
    gate_ref,
    result_ref,
    grad_inputs_ref,
    *rest,
):
    projected_grad_ref = rest[-1]
    blocks = inputs_ref.shape[0] // SLOT
    grad_out = grad_out_ref[...]
    gate = gate_ref[...]
    grad_gate = jnp.sum(grad_out * result_ref[...], axis=-1, keepdims=True)
    names = lax.broadcasted_iota(jnp.int32, (1, router_ref.shape[0]), 1)
    choose = jnp.where(names == route_ref[...], 1.0, 0.0)
    grad_logits = (grad_gate * gate * (choose - route_probs_ref[...])).astype(bf16)
    slots = lax.broadcasted_iota(jnp.int32, (1, returned_ref.shape[0]), 1)
    placing = jnp.where(slots == target_ref[...], 1.0, 0.0).astype(bf16)
    grad_routed = dot(placing, returned_ref[...]) + dot(grad_logits, router_ref[...])
    middle = middle_ref[...]
    grad_middle_norm, grad_gain_two = norm_backward(grad_routed, middle, gains_ref[1:2])
    grad_middle = grad_out + grad_middle_norm
    grad_branch = grad_middle.astype(bf16)
    grad_attended = dot_nt(grad_branch, weight_ref[:, 3 * D :]).astype(bf16)
    low, first, second = lane_masks()
    width = 2 * HEAD_DIM
    scale_qk = HEAD_DIM ** (-0.5)
    places = [lax.broadcasted_iota(jnp.int32, (SLOT, SLOT), axis) for axis in range(2)]
    reverse = jnp.where(places[0] + places[1] == SLOT - 1, 1.0, 0.0).astype(bf16)
    for pair in range(HEADS // 2):
        scores_total = jnp.zeros((2 * SLOT, SLOT), f32)
        for block in range(blocks):
            rows = slice(block * SLOT, (block + 1) * SLOT)
            columns = [
                slice(part * D + pair * width, part * D + (pair + 1) * width) for part in range(3)
            ]
            queries, keys, values = [projected_ref[rows, part] for part in columns]
            grads = both_heads(
                grad_attended[rows, pair * width : (pair + 1) * width], first, second
            )
            probs = probs_ref[block, pair]
            grad_probs = dot_nt(grads, values)
            grad_scores = (
                probs * (grad_probs - jnp.sum(probs * grad_probs, axis=-1, keepdims=True))
            ).astype(bf16)
            projected_grad_ref[rows, columns[0]] = (
                own_lanes(low, dot(grad_scores, keys)) * scale_qk
            ).astype(bf16)
            projected_grad_ref[rows, columns[1]] = (
                dot_tn(grad_scores, both_heads(queries, first, second)) * scale_qk
            ).astype(bf16)
            projected_grad_ref[rows, columns[2]] = dot_tn(probs.astype(bf16), grads).astype(bf16)
            if full:
                scores_total = scores_total + jnp.concatenate(
                    [dot(reverse, grad_scores[:SLOT]), dot(reverse, grad_scores[SLOT:])], axis=0
                )
        if full:
            for own in range(2):
                part = scores_total[own * SLOT : (own + 1) * SLOT]
                wide = jnp.concatenate([part, jnp.zeros_like(part)], axis=1)
                moved = pltpu.roll(wide, 1, 1, stride=1, stride_axis=0)
                rest[2][2 * pair + own : 2 * pair + own + 1] = jnp.sum(
                    moved, axis=0, keepdims=True
                )
    inputs = inputs_ref[...]
    grad_normed = dot_nt(projected_grad_ref[...], weight_ref[:, : 3 * D])
    grad_inputs_norm, grad_gain_one = norm_backward(grad_normed, inputs, gains_ref[0:1])
    grad_inputs_ref[...] = grad_middle + grad_inputs_norm
    if full:
        dense_ref, small_ref = rest[0], rest[1]
        normed = (inputs * rms_scale(inputs) * gains_ref[0:1]).astype(bf16)
        routed = (middle * rms_scale(middle) * gains_ref[1:2]).astype(bf16)
        for part in range(3):
            columns = slice(part * D, (part + 1) * D)
            dense_ref[:, columns] = dot_tn(normed, projected_grad_ref[:, columns]).astype(bf16)
        dense_ref[:, 3 * D :] = dot_tn(attended_ref[...], grad_branch).astype(bf16)
        small_ref[0:1] = grad_gain_one[None]
        small_ref[1:2] = grad_gain_two[None]
        small_ref[8:] = dot_tn(grad_logits, routed)[:experts]


def front_call(inputs, dense, fixed):
    gains, weight, router, diagonals = dense
    same_seq, route_ids, targets, placing = fixed
    extent = inputs.shape[0]
    experts = lax.axis_size("dp") // 2
    shape = jax.ShapeDtypeStruct
    return pl.pallas_call(
        functools.partial(front_kernel, experts),
        out_shape=(
            shape((placing.shape[1], D), bf16),
            shape((extent, 3 * D), bf16),
            shape((extent // SLOT, HEADS // 2, 2 * SLOT, SLOT), f32),
            shape((extent, D), bf16),
            shape((extent, D), f32),
            shape((extent, router.shape[0]), f32),
            shape((extent, 1), f32),
        ),
        compiler_params=pltpu.CompilerParams(vmem_limit_bytes=50 * 1024 * 1024),
        cost_estimate=pl.CostEstimate(
            flops=2 * extent * D * 4 * D, bytes_accessed=12_000_000, transcendentals=400_000
        ),
        name="attention_front",
    )(inputs, gains, weight, router, diagonals, same_seq, route_ids[:, None], targets[None, :])


def back_call(grad_out, returned, kept, dense, fixed, full):
    gains, weight, router, diagonals = dense
    same_seq, route_ids, targets, placing = fixed
    inputs, projected, probs, attended, middle, route_probs, gate, result = kept
    extent = inputs.shape[0]
    experts = lax.axis_size("dp") // 2
    shape = jax.ShapeDtypeStruct
    out_shape = [shape((extent, D), f32)]
    if full:
        out_shape = out_shape + [
            shape((D, 4 * D), bf16),
            shape((8 + experts, D), f32),
            shape((HEADS, 2 * SLOT), f32),
        ]
    return pl.pallas_call(
        functools.partial(back_kernel, experts, full),
        out_shape=tuple(out_shape),
        scratch_shapes=[pltpu.VMEM((extent, 3 * D), bf16)],
        compiler_params=pltpu.CompilerParams(vmem_limit_bytes=50 * 1024 * 1024),
        cost_estimate=pl.CostEstimate(
            flops=4 * extent * D * 4 * D, bytes_accessed=20_000_000, transcendentals=1000
        ),
        name="attention_back_full" if full else "attention_back",
    )(
        grad_out,
        returned,
        targets[:, None],
        route_ids[:, None],
        inputs,
        gains,
        weight,
        router,
        projected,
        probs,
        attended,
        middle,
        route_probs,
        gate,
        result,
    )


def gelu_parts(hidden):
    rate, cubic = 0.7978845608028654, 0.044715
    squared = hidden * hidden
    bend = jnp.tanh(rate * hidden * (1.0 + cubic * squared))
    active = 0.5 * hidden * (1.0 + bend)
    slope = 0.5 * (1.0 + bend) + 0.5 * hidden * (1.0 - bend * bend) * rate * (
        1.0 + 3.0 * cubic * squared
    )
    return (active.astype(bf16), slope.astype(bf16))


def layer_forward(inputs, dense, fixed, experts_held):
    placing = fixed[-1]
    weight_in, weight_out = experts_held
    packed, projected, probs, attended, middle, route_probs, gate = front_call(
        inputs, dense, fixed
    )
    arrived = to_experts(packed)
    active, slope = zip(*[gelu_parts(dot(rows, weight_in)) for rows in arrived])
    replies = [dot(rows, weight_out) for rows in active]
    result = dot(placing, from_experts(replies[0], replies[1]))
    outputs = middle + gate * result
    kept = (inputs, projected, probs, attended, middle, route_probs, gate, result)
    return (outputs, kept, (arrived, active, slope))


def layer_backward(grad_out, kept, expert_kept, dense, fixed, experts_held, full):
    arrived, active, slope = expert_kept
    placing = fixed[-1]
    weight_in, weight_out = experts_held
    grad_result = (kept[6] * grad_out).astype(bf16)
    grad_rows = to_experts(
        jnp.einsum("ts,td->sd", placing, grad_result, preferred_element_type=f32).astype(bf16)
    )
    grad_hidden = [
        (
            jnp.einsum("rd,fd->rf", rows, weight_out, preferred_element_type=f32)
            * steep.astype(f32)
        ).astype(bf16)
        for rows, steep in zip(grad_rows, slope)
    ]
    grad_sent = [
        jnp.einsum("rf,df->rd", rows, weight_in, preferred_element_type=f32)
        for rows in grad_hidden
    ]
    returned = from_experts(grad_sent[0], grad_sent[1])
    outs = back_call(grad_out, returned, kept, dense, fixed, full)
    if not full:
        return outs[0]
    grad_expert_out = jnp.einsum(
        "krf,krd->fd", jnp.stack(active), jnp.stack(grad_rows), preferred_element_type=f32
    )
    grad_expert_in = jnp.einsum(
        "krd,krf->df", jnp.stack(arrived), jnp.stack(grad_hidden), preferred_element_type=f32
    )
    return (*outs, grad_expert_in, grad_expert_out)


def pack_small(gains, router, table):
    rows = 8 + router.shape[1]
    packed = jnp.zeros((rows + -rows % 16, 128), bf16)
    packed = packed.at[0:2, : gains.shape[1]].set(gains)
    packed = packed.at[2, : table.shape[0]].set(table)
    return packed.at[8:rows, : router.shape[0]].set(router.T)


def unpack_small(packed, devices, experts):
    extent = D // devices
    packed = packed.reshape(devices, -1, 128).swapaxes(0, 1)
    gains = packed[0:2, :, :extent].reshape(2, D).astype(f32)
    table = packed[2, :, : BUCKETS * HEADS // devices].reshape(BUCKETS, HEADS).astype(f32)
    router = packed[8 : 8 + experts, :, :extent].reshape(experts, D)
    return (gains, table, jnp.pad(router, ((0, -experts % 128), (0, 0))))


def scatter_dense(packed):
    devices = lax.axis_size("dp")
    core = lax.axis_index("dp") % 2
    packed = packed.reshape(devices // 2, 2, D // devices, -1)
    mine = lax.dynamic_index_in_dim(packed, core, axis=1, keepdims=False)
    others = lax.dynamic_index_in_dim(packed, 1 - core, axis=1, keepdims=False)
    summed = (mine.astype(f32) + pair_swap(others).astype(f32)).astype(bf16)
    return jnp.sum(chip_all_to_all(summed).astype(f32), axis=0)


def scatter_small(small, table, devices):
    entries = jnp.pad(
        table.reshape(devices, -1), ((0, 0), (0, D // devices - table.size // devices))
    )
    small = small.at[2].set(entries.reshape(-1))
    small = small.reshape(-1, devices, D // devices).swapaxes(0, 1)
    small = jnp.pad(small, ((0, 0), (0, 0), (0, 128 - D // devices)))
    total = jnp.sum(
        lax.all_to_all(small, "dp", split_axis=0, concat_axis=0, tiled=True), axis=0
    )
    return (
        total[0:2, : D // devices],
        total[8:, : D // devices].T,
        total[2, : table.size // devices],
    )


def shards(
    edge_rows,
    lengths,
    routes,
    norm_gains,
    qkv_weight,
    out_weight,
    router_weight,
    bias_table,
    expert_in,
    expert_out,
):
    devices = lax.axis_size("dp")
    experts = devices // 2
    first_section = lax.axis_index("section") == 0
    local_rows = edge_rows[0].astype(f32)
    onehot = bucket_onehot()
    experts_held = (expert_in[0], expert_out[0])
    weight = lax.all_gather(
        jnp.concatenate([qkv_weight[0], out_weight[0]], axis=1), "dp", axis=0, tiled=True
    )
    small = lax.all_gather(
        pack_small(norm_gains[0], router_weight[0], bias_table[0]), "dp", axis=0, tiled=True
    )
    gains, table, router = unpack_small(small, devices, experts)
    diagonals = jnp.einsum("ib,bh->hi", onehot, table, precision=lax.Precision.HIGHEST)
    dense = (gains, weight, router, diagonals)
    route_ids = routes[0, :, 0]
    targets, placing = expert_places(route_ids.reshape(-1, SLOT), experts, 4 * SLOT // devices)
    fixed = (same_sequence(lengths), route_ids, targets, placing)
    outputs, _, _ = layer_forward(local_rows, dense, fixed, experts_held)
    carried = section_shift(outputs.astype(bf16), 1).astype(f32)
    inputs = jnp.where(first_section, local_rows, carried)
    outputs, kept, expert_kept = layer_forward(inputs, dense, fixed, experts_held)
    grad_inputs = layer_backward(
        local_rows, kept, expert_kept, dense, fixed, experts_held, False
    )
    carried = section_shift(grad_inputs.astype(bf16), -1).astype(f32)
    grad_out = jnp.where(first_section, carried, local_rows)
    grad_inputs, dense_grads, small_grads, diagonal_grads, grad_in, grad_exp_out = layer_backward(
        grad_out, kept, expert_kept, dense, fixed, experts_held, True
    )
    edge_results = jnp.where(first_section, grad_inputs, outputs)
    grad_table = jnp.einsum(
        "ib,hi->bh", onehot, diagonal_grads, precision=lax.Precision.HIGHEST
    ).reshape(-1)
    grad_gains, grad_router, grad_table = scatter_small(small_grads, grad_table, devices)
    total = scatter_dense(dense_grads)
    return (
        edge_results[None],
        grad_gains[None],
        total[None, :, : 3 * D],
        total[None, :, 3 * D :],
        grad_router[None],
        grad_table[None],
        grad_in[None],
        grad_exp_out[None],
    )


def solution(mesh):
    return jax.shard_map(
        shards,
        mesh=mesh,
        in_specs=(
            P("section", "dp", None),
            P("dp", None),
            P("section", "dp", None),
            P("section", None, "dp"),
            P("section", "dp", None),
            P("section", "dp", None),
            P("section", "dp", None),
            P("section", "dp"),
            P("section", None, "dp"),
            P("section", "dp", None),
        ),
        out_specs=(
            P("section", "dp", None),
            P("section", None, "dp"),
            P("section", "dp", None),
            P("section", "dp", None),
            P("section", "dp", None),
            P("section", "dp"),
            P("section", None, "dp"),
            P("section", "dp", None),
        ),
        check_vma=False,
    )
```

time: 558 us -> 477 us (0.85)
  matrix products: 134 us -> 66.8 us
  local copies, waits for them, and re-layouts: 75.7 us -> 30.4 us
  Pallas kernels: 0 us -> 39.5 us
  waiting for transfers between devices: 186 us -> 161 us
  blocking collectives: 71.8 us -> 95.3 us
  other arithmetic: 32.8 us -> 23.1 us
    dot_general x27 -> x4, matrix products: 52.7 us -> 2.57 us  [the longest x2 2.07 us: layer_backward(): jnp.einsum('ts,td->sd', placing, grad_result, preferred_element_type=f32)]
    pallas_call x0 -> x4, Pallas kernels: none -> 39.5 us  [the longest x2 24.8 us: back_call(): pl.pallas_call(functools.partial(back_kernel, experts, full), out_shape=t...]
    all_gather x1, waiting for transfers between devices: 51 us -> 25.6 us  [shards(): lax.all_gather(jnp.concatenate([qkv_weight[0], out_weight[0]], axis=1), '...]
    all_gather x0 -> x1, blocking collectives: none -> 23.5 us  [shards(): lax.all_gather(pack_small(norm_gains[0], router_weight[0], bias_table[0])...]
    dot_general x16 -> x8, matrix products: 47.7 us -> 30.2 us  [dot(): return jnp.dot(lhs, rhs, preferred_element_type=f32)]
    reshape x11 -> x4, local copies, waits for them, and re-layouts: 17.1 us -> 0.27 us  [the longest x2 0.15 us: scatter_small(): small = small.reshape(-1, devices, D // devices).swapaxes(0, 1)]
    split x8 -> x0, local copies, waits for them, and re-layouts: 13.6 us -> none  [layer_forward(): jnp.split(projected, 3, axis=-1)]
    convert_element_type x11 -> x1, local copies, waits for them, and re-layouts: 11.6 us -> 0.08 us  [unpack_small(): gains = packed[0:2, :, :extent].reshape(2, D).astype(f32)]
  transfers between devices with their start and end apart: 18 -> 19, of which waited for: 13 -> 13; matrix products, arithmetic and copies ran while one was open for 14% -> 16% of each run, Pallas kernels for 0% -> 0%
where the time goes in v2:
time: 477 us; the launch traced here: 468 us
  waiting for transfers between devices  161 us (34%)
  blocking collectives  95.3 us (20%)
  matrix products  66.8 us (14%)
  Pallas kernels  39.5 us (8%)
  starting transfers between devices  37.4 us (8%)
  local copies, waits for them, and re-layouts  30.4 us (6%)
  other arithmetic  23.1 us (5%)
  between operations  15.1 us (3%)
    all_to_all x6, waiting for transfers between devices, chip_all_to_all(): lax.all_to_all(block, 'dp', split_axis=0, concat_axis=0, tiled=True, axis...  109 us
    all_to_all x3, blocking collectives, chip_all_to_all(): lax.all_to_all(block, 'dp', split_axis=0, concat_axis=0, tiled=True, axis...  71.7 us
    dot_general x8, matrix products, dot(): return jnp.dot(lhs, rhs, preferred_element_type=f32)  30.2 us
    all_to_all x6, starting transfers between devices, chip_all_to_all(): lax.all_to_all(block, 'dp', split_axis=0, concat_axis=0, tiled=True, axis...  25.7 us
    all_gather x1, waiting for transfers between devices, shards(): lax.all_gather(jnp.concatenate([qkv_weight[0], out_weight[0]], axis=1), '...  25.6 us
    pallas_call x2, Pallas kernels, back_call(): pl.pallas_call(functools.partial(back_kernel, experts, full), out_shape=t...  24.8 us
    all_gather x1, blocking collectives, shards(): lax.all_gather(pack_small(norm_gains[0], router_weight[0], bias_table[0])...  23.5 us
    dot_general x4, matrix products, layer_backward(): jnp.einsum('rf,df->rd', rows, weight_in, preferred_element_type=f32)  17.9 us
  transfers between devices with their start and end apart: 19, of which 13 were waited for; matrix products, arithmetic and copies ran while one was open for 16% of the time, Pallas kernels for 0%

profile of v2, /device:TPU:0, one launch (start us, length us, event | category | flops | bytes accessed | tf_op | source)
XLA Modules:
  0.0 468.4 jit_solution(16271000668845966512)
XLA Ops:
  12.1 23.5 %all_gather.6 = bf16[256,128]{1,0:T(8,128)(2,1)S(1)} all-gather(bf16[16,128]{1,0:T(8,128)(2,1)S(1)} %scatter.16), channel_id=1, replica_groups=mesh['section'=2,'dp'=16] {'dp'}, dimensions={0}, use_global_device_ids=true | all-gather | bytes 69632 | tf_op jit(solution)/shard_map/all_gather | solution.py:484
  41.6 25.6 %all-gather.2.cloned.1.call-done.weight_ref = bf16[768,3072]{1,0:T(8,128)(2,1)} async-done(((bf16[48,3072]{1,0:T(8,128)(2,1)}), bf16[768,3072]{1,0:T(8,128)(2,1)}) %all-gather.2.cloned.1.call-update) | async-done | bytes 4718608 | tf_op jit(solution)/shard_map/all_gather | solution.py:481
  68.1 7.2 %attention_front.2 = (bf16[512,768]{1,0:T(8,128)(2,1)S(1)}, bf16[256,2304]{1,0:T(8,128)(2,1)}, f32[2,6,256,128]{3,2,1,0:T(8,128)}, bf16[256,768]{1,0:T(8,128)(2,...) custom-call(f32[256,768]{1,0:T(8,128)S(1)} %bitcast_convert_fusion.inputs_ref.grad_out_ref, ...), custom_call_target="tpu_custom_call" | custom-call | flops 1207959552 | bytes 12000000 | tf_op jit(solution)/shard_map/attention_front/pallas_call | solution.py:300
  75.4 23.5 %all_to_all.50 = bf16[8,64,768]{2,1,0:T(8,128)(2,1)S(1)} all-to-all(bf16[8,64,768]{2,1,0:T(8,128)(2,1)S(1)} %bitcast.179), channel_id=1, replica_groups={{0,2,4,6,8,10,12,14},{1,3,5,7,9,11,13,15},{16,18,20,22,24,26,28,30},{17..., dimensions={0} | all-to-all | bytes 1572864 | tf_op jit(solution)/shard_map/all_to_all | solution.py:41
  101.2 5.4 %fusion.55 = bf16[512,768]{1,0:T(8,128)(2,1)} fusion(bf16[1,1536,768]{2,1,0:T(8,128)(2,1)S(1)} %copy-done, bf16[512,768]{1,0:T(8,128)(2,1)S(1)} %collective-permute-done, bf16[1,768,1536]{2,1,0:T(8,128)(2,1)} %param.26), kind=kOutput, calls=%fused_computation.68 | convolution fusion | flops 2423390208 | bytes 6291456 | tf_op jit(solution)/shard_map/dot_general | solution.py:25
  106.7 2.5 collective-permute-done.1
  109.2 5.8 %add_convert_fusion.5 = bf16[512,768]{1,0:T(8,128)(2,1)} fusion(bf16[512,768]{1,0:T(8,128)(2,1)} %collective-permute-done.1, bf16[1,1536,768]{2,1,0:T(8,128)(2,1)S(1)} %copy-done, bf16[512,768]{1,0:T(8,128)(2,1)} %bitcast.193, bf16[1,768,1536]{2,1,0:T(8,128)(2,1)} %param.26), kind=kOutput, calls=%fused_computation.65 | convolution fusion | flops 2424176640 | bytes 7077888 | tf_op jit(solution)/shard_map/dot_general | solution.py:25
  114.9 4.3 all-to-all-start.1
  119.5 20.6 %all-to-all-done.1 = bf16[8,64,768]{2,1,0:T(8,128)(2,1)} async-done(((bf16[8,64,768]{2,1,0:T(8,128)(2,1)}), bf16[8,64,768]{2,1,0:T(8,128)(2,1)}, u32[]{:S(2)}, u32[]{:S(2)}) %all-to-all-start.1) | async-done | bytes 786464 | tf_op jit(solution)/shard_map/all_to_all | solution.py:41
  140.0 2.5 fusion.62
  142.6 4.6 collective-permute-start.2
  147.1 6.9 %collective-permute-done.2 = bf16[256,768]{1,0:T(8,128)(2,1)} collective-permute-done((bf16[256,768]{1,0:T(8,128)(2,1)}, bf16[256,768]{1,0:T(8,128)(2,1)}, u32[]{:S(2)}, u32[]{:S(2)}) %collective-permute-start.2) | collective-permute-done | bytes 393248 | tf_op jit(solution)/shard_map/ppermute | solution.py:31
  155.2 7.4 %attention_front.3 = (bf16[512,768]{1,0:T(8,128)(2,1)S(1)}, bf16[256,2304]{1,0:T(8,128)(2,1)}, f32[2,6,256,128]{3,2,1,0:T(8,128)}, bf16[256,768]{1,0:T(8,128)(2,...) custom-call(f32[256,768]{1,0:T(8,128)S(1)} %convert_select_fusion.1.inputs_ref, ...), custom_call_target="tpu_custom_call" | custom-call | flops 1207959552 | bytes 12000000 | tf_op jit(solution)/shard_map/attention_front/pallas_call | solution.py:300
  164.2 23.7 %all_to_all.51 = bf16[8,64,768]{2,1,0:T(8,128)(2,1)} all-to-all(bf16[8,64,768]{2,1,0:T(8,128)(2,1)S(1)} %bitcast.178), channel_id=1, replica_groups={{0,2,4,6,8,10,12,14},{1,3,5,7,9,11,13,15},{16,18,20,22,24,26,28,30},{17..., dimensions={0} | all-to-all | bytes 1572864 | tf_op jit(solution)/shard_map/all_to_all | solution.py:41
  188.0 2.3 copy.65
  191.8 4.2 all-to-all-start.2
  196.1 3.3 fusion.29
  199.4 2.8 fusion.58
  202.8 14.4 %all-to-all-done.2 = bf16[8,64,768]{2,1,0:T(8,128)(2,1)} async-done(((bf16[8,64,768]{2,1,0:T(8,128)(2,1)}), bf16[8,64,768]{2,1,0:T(8,128)(2,1)}, u32[]{:S(2)}, u32[]{:S(2)}) %all-to-all-start.2) | async-done | bytes 786464 | tf_op jit(solution)/shard_map/all_to_all | solution.py:41
  217.2 3.3 fusion.33
  220.5 4.6 add_convert_fusion.3
  225.1 4.4 all-to-all-start.5
  229.5 6.9 %fusion.49 = bf16[512,768]{1,0:T(8,128)(2,1)} fusion(bf16[1,768,1536]{2,1,0:T(8,128)(2,1)} %param.26, bf16[512,768]{1,0:T(8,128)(2,1)S(1)} %collective-permute-done.3, bf16[1,1536,768]{2,1,0:T(8,128)(2,1)S(1)} %copy-done, f32[512,1536]{1,0:T(8,128)} %copy-done.24), kind=kOutput, calls=%fused_computation.66 | convolution fusion | flops 2432040960 | bytes 9437184 | tf_op jit(solution)/shard_map/rf,df->rd/dot_general | solution.py:403
  236.9 7.3 %fusion.31 = f32[512,768]{1,0:T(8,128)} fusion(bf16[1,768,1536]{2,1,0:T(8,128)(2,1)} %param.26, bf16[512,768]{1,0:T(8,128)(2,1)} %bitcast.26, bf16[1,1536,768]{2,1,0:T(8,128)(2,1)S(1)} %copy-done, f32[512,1536]{1,0:T(8,128)} %copy-done.31), kind=kOutput, calls=%fused_computation.47 | convolution fusion | flops 2431647744 | bytes 10223616 | tf_op jit(solution)/shard_map/rf,df->rd/dot_general | solution.py:403
  244.1 2.8 add_convert_fusion.4
  246.9 3.7 all-to-all-done.5
  250.6 4.2 all-to-all-start.4
  258.0 2.5 fusion.78.result_ref
  260.5 14.6 %all-to-all-done.4 = bf16[8,64,768]{2,1,0:T(8,128)(2,1)} async-done(((bf16[8,64,768]{2,1,0:T(8,128)(2,1)}), bf16[8,64,768]{2,1,0:T(8,128)(2,1)}, u32[]{:S(2)}, u32[]{:S(2)}) %all-to-all-start.4) | async-done | bytes 786464 | tf_op jit(solution)/shard_map/all_to_all | solution.py:41
  278.8 10.5 %attention_back.1 = f32[256,768]{1,0:T(8,128)S(1)} custom-call(f32[256,768]{1,0:T(8,128)S(1)} %copy-done.5, bf16[512,768]{1,0:T(8,128)(2,1)} %bitcast.30.returned_ref, s32[256,1]{1,0:T(8,128)S(1)} %copy-done.12, s32[256,1]{1,0:T(8,128)S(1)} %copy.63.route_ref, f32[256,768]{1,0:T(8,128)} %copy-done.1, f32[2,768]{1,0:T(2,128)S(1)} %reshape.357.gains_ref, ...), custom_call_target="tpu_custom_call" | custom-call | flops 2415919104 | bytes 20000000 | tf_op jit(solution)/shard_map/attention_back/pallas_call | solution.py:333
  291.0 10.4 %collective-permute-done.7 = bf16[256,768]{1,0:T(8,128)(2,1)S(1)} collective-permute-done((bf16[256,768]{1,0:T(8,128)(2,1)S(1)}, bf16[256,768]{1,0:T(8,128)(2,1)S(1)}, u32[]{:S(2)}, u32[]{:S(2)}) %collective-permute-start.7) | collective-permute-done | bytes 393248 | tf_op jit(solution)/shard_map/ppermute | solution.py:31
  302.1 24.5 %all_to_all.52 = bf16[8,64,768]{2,1,0:T(8,128)(2,1)S(1)} all-to-all(bf16[8,64,768]{2,1,0:T(8,128)(2,1)S(1)} %bitcast.186), channel_id=1, replica_groups={{0,2,4,6,8,10,12,14},{1,3,5,7,9,11,13,15},{16,18,20,22,24,26,28,30},{17..., dimensions={0} | all-to-all | bytes 1572864 | tf_op jit(solution)/shard_map/all_to_all | solution.py:41
  326.6 2.3 collective-permute-done.8
  328.9 2.7 fusion.10
  334.1 2.7 fusion.8
  336.8 2.3 add_convert_fusion.2
  339.1 4.2 all-to-all-start.7
  343.4 20.7 %all-to-all-done.7 = bf16[8,64,768]{2,1,0:T(8,128)(2,1)} async-done(((bf16[8,64,768]{2,1,0:T(8,128)(2,1)}), bf16[8,64,768]{2,1,0:T(8,128)(2,1)}, u32[]{:S(2)}, u32[]{:S(2)}) %all-to-all-start.7) | async-done | bytes 786464 | tf_op jit(solution)/shard_map/all_to_all | solution.py:41
  367.8 14.3 %attention_back_full.1 = (f32[256,768]{1,0:T(8,128)S(1)}, bf16[768,3072]{1,0:T(8,128)(2,1)}, f32[16,768]{1,0:T(8,128)S(1)}, f32[12,256]{1,0:T(8,128)S(1)}) custom-call(f32[256,768]{1,0:T(8,128)S(1)} %convert_select_fusion.grad_out_ref, bf16[512,768]{1,0:T(8,128)(2,1)} %bitcast.38.returned_ref, s32[256,1]{1,0:T(8,128)S(1)} %copy-done.13, ...), custom_call_target="tpu_custom_call" | custom-call | flops 2415919104 | bytes 20000000 | tf_op jit(solution)/shard_map/attention_back_full/pallas_call | solution.py:333
  383.0 3.2 dynamic-slice_bitcast_fusion
  387.6 4.1 all-to-all-start.8
  391.7 4.7 %fusion = bf16[8,48,3072]{2,1,0:T(8,128)(2,1)} fusion(bf16[8,48,3072]{2,1,0:T(8,128)(2,1)} %collective-permute-done.10, bf16[8,2,48,3072]{3,2,1,0:T(8,128)(2,1)} %bitcast.184, s32[]{:T(128)S(6)} %select_n.35), kind=kLoop, calls=%fused_computation.1 | loop fusion | flops 4718592 | bytes 7077892 | tf_op jit(solution)/shard_map/convert_element_type | solution.py:442
  396.4 3.2 all-to-all-done.8
  399.6 4.4 all-to-all-start.9
  405.1 3.0 fusion.124
  410.3 5.5 %convolution_bitcast_fusion.1 = f32[1,768,1536]{2,1,0:T(8,128)} fusion(bf16[1,512,1536]{2,1,0:T(8,128)(2,1)S(1)} %bitcast.212, bf16[1,512,1536]{2,1,0:T(8,128)(2,1)S(1)} %bitcast.213, bf16[1,512,768]{1,2,0:T(8,128)(2,1)} %bitcast.50, bf16[1,512,768]{1,2,0:T(8,128)(2,1)S(1)} %copy-done.37), kind=kOutput, calls=%fused_computation.8 | convolution fusion | flops 2418278400 | bytes 9437184 | tf_op jit(solution)/shard_map/krd,krf->df/dot_general | solution.py:413
  415.8 4.4 convolution_bitcast_fusion
  423.0 34.6 %all-to-all-done.9 = bf16[8,48,3072]{2,1,0:T(8,128)(2,1)} async-done(((bf16[8,48,3072]{2,1,0:T(8,128)(2,1)}), bf16[8,48,3072]{2,1,0:T(8,128)(2,1)}, u32[]{:S(2)}, u32[]{:S(2)}) %all-to-all-start.9) | async-done | bytes 2359328 | tf_op jit(solution)/shard_map/all_to_all | solution.py:41
  (164 shorter events, 46.9 us)
Async XLA Ops:
  7.2 94.0 %copy-start = (bf16[1,1536,768]{2,1,0:T(8,128)(2,1)S(1)}, bf16[1,1536,768]{2,1,0:T(8,128)(2,1)}, u32[]{:S(2)}) copy-start(bf16[1,1536,768]{2,1,0:T(8,128)(2,1)} %param.27) | copy-start | bytes 7077892
  7.2 60.0 %all-gather.2.cloned.1.call-start = ((), (), s32[]{:S(2)}) async-start(), calls=%async_computation.10 | async-start | bytes 5013504 | tf_op jit(solution)/shard_map/all_gather | solution.py:481
  41.6 57.2 %copy-start.4 = (f32[256,768]{1,0:T(8,128)}, f32[256,768]{1,0:T(8,128)S(1)}, u32[]{:S(2)}) copy-start(f32[256,768]{1,0:T(8,128)S(1)} %bitcast_convert_fusion.inputs_ref.grad_out_ref) | copy-start | bytes 2359300
  75.4 23.5 %copy-start.16 = (f32[256,768]{1,0:T(8,128)}, f32[256,768]{1,0:T(8,128)S(1)}, u32[]{:S(2)}) copy-start(f32[256,768]{1,0:T(8,128)S(1)} %get-tuple-element.70) | copy-start | bytes 2359300
  75.4 23.6 %copy-start.22 = (f32[256,1]{1,0:T(8,128)}, f32[256,1]{1,0:T(8,128)S(1)}, u32[]{:S(2)}) copy-start(f32[256,1]{1,0:T(8,128)S(1)} %get-tuple-element.71) | copy-start | bytes 3076
  98.8 2.3 collective-permute-start
  106.6 12.7 %copy-start.38 = (s32[1,256,1]{1,2,0:T(1,128)S(1)}, s32[1,256,1]{1,2,0:T(1,128)}, u32[]{:S(2)}) copy-start(s32[1,256,1]{1,2,0:T(1,128)} %param.20) | copy-start | bytes 3076
  106.6 12.8 %copy-start.23 = (f32[256,1]{1,0:T(8,128)S(1)}, f32[256,1]{1,0:T(8,128)}, u32[]{:S(2)}) copy-start(f32[256,1]{1,0:T(8,128)} %copy-done.22) | copy-start | bytes 3076
  106.6 2.6 collective-permute-start.1
  114.9 39.1 %copy-start.29 = (bf16[1,256,768]{2,1,0:T(8,128)(2,1)S(1)}, bf16[1,256,768]{2,1,0:T(8,128)(2,1)}, u32[]{:S(2)}) copy-start(bf16[1,256,768]{2,1,0:T(8,128)(2,1)} %param.18) | copy-start | bytes 1179652
  114.9 40.2 %copy-start.15 = (f32[2,128,128]{2,1,0:T(8,128)S(1)}, f32[2,128,128]{2,1,0:T(8,128)}, u32[]{:S(2)}) copy-start(f32[2,128,128]{2,1,0:T(8,128)} %compare_convert_fusion.same_ref) | copy-start | bytes 393220
  114.9 25.1 %all-to-all-start.1 = ((bf16[8,64,768]{2,1,0:T(8,128)(2,1)}), bf16[8,64,768]{2,1,0:T(8,128)(2,1)}, u32[]{:S(2)}, u32[]{:S(2)}) async-start(bf16[8,64,768]{2,1,0:T(8,128)(2,1)} %bitcast.194), calls=%async_computation.1 | async-start | bytes 1572864 | tf_op jit(solution)/shard_map/all_to_all | solution.py:41
  142.6 11.5 %collective-permute-start.2 = (bf16[256,768]{1,0:T(8,128)(2,1)}, bf16[256,768]{1,0:T(8,128)(2,1)}, u32[]{:S(2)}, u32[]{:S(2)}) collective-permute-start(bf16[256,768]{1,0:T(8,128)(2,1)} %fusion.62), channel_id=1, source_target_pairs={{0,16},{1,17},{2,18},{3,19},{4,20},{5,21},{6,22},{7,23},{8,24},{9,... | collective-permute-start | bytes 1179656 | tf_op jit(solution)/shard_map/ppermute | solution.py:31
  155.2 32.8 %copy-start.1 = (f32[256,768]{1,0:T(8,128)}, f32[256,768]{1,0:T(8,128)S(1)}, u32[]{:S(2)}) copy-start(f32[256,768]{1,0:T(8,128)S(1)} %convert_select_fusion.1.inputs_ref) | copy-start | bytes 2359300
  164.2 23.7 %copy-start.19 = (f32[256,128]{1,0:T(8,128)}, f32[256,128]{1,0:T(8,128)S(1)}, u32[]{:S(2)}) copy-start(f32[256,128]{1,0:T(8,128)S(1)} %get-tuple-element.79.route_probs_ref) | copy-start | bytes 393220
  164.2 35.2 %copy-start.9 = (f32[256,1]{1,0:T(8,128)}, f32[256,1]{1,0:T(8,128)S(1)}, u32[]{:S(2)}) copy-start(f32[256,1]{1,0:T(8,128)S(1)} %get-tuple-element.73.gate_ref) | copy-start | bytes 3076
  190.3 5.8 %collective-permute-start.4 = (bf16[512,768]{0,1:T(8,128)(2,1)}, bf16[512,768]{0,1:T(8,128)(2,1)}, u32[]{:S(2)}, u32[]{:S(2)}) collective-permute-start(bf16[512,768]{0,1:T(8,128)(2,1)} %copy.65), channel_id=1, source_target_pairs={{0,1},{1,0},{2,3},{3,2},{4,5},{5,4},{6,7},{7,6},{8,9},{9,8},{10,11... | collective-permute-start | bytes 2359304 | tf_op jit(solution)/shard_map/ppermute | solution.py:35
  191.8 25.3 %all-to-all-start.2 = ((bf16[8,64,768]{2,1,0:T(8,128)(2,1)}), bf16[8,64,768]{2,1,0:T(8,128)(2,1)}, u32[]{:S(2)}, u32[]{:S(2)}) async-start(bf16[8,64,768]{2,1,0:T(8,128)(2,1)} %bitcast.185), calls=%async_computation.2 | async-start | bytes 1572864 | tf_op jit(solution)/shard_map/all_to_all | solution.py:41
  199.4 2.9 copy-start.24
  202.3 18.2 %collective-permute-start.6 = (bf16[512,768]{1,0:T(8,128)(2,1)}, bf16[512,768]{1,0:T(8,128)(2,1)}, u32[]{:S(2)}, u32[]{:S(2)}) collective-permute-start(bf16[512,768]{1,0:T(8,128)(2,1)} %fusion.58), channel_id=1, source_target_pairs={{0,1},{1,0},{2,3},{3,2},{4,5},{5,4},{6,7},{7,6},{8,9},{9,8},{10,11... | collective-permute-start | bytes 2359304 | tf_op jit(solution)/shard_map/ppermute | solution.py:35
  217.2 12.3 %collective-permute-start.3 = (bf16[512,768]{1,0:T(8,128)(2,1)}, bf16[512,768]{1,0:T(8,128)(2,1)S(1)}, u32[]{:S(2)}, u32[]{:S(2)}) collective-permute-start(bf16[512,768]{1,0:T(8,128)(2,1)} %bitcast.26), channel_id=1, source_target_pairs={{0,1},{1,0},{2,3},{3,2},{4,5},{5,4},{6,7},{7,6},{8,9},{9,8},{10,11... | collective-permute-start | bytes 2359304 | tf_op jit(solution)/shard_map/ppermute | solution.py:35
  220.5 4.6 copy-start.31
  225.1 25.5 %all-to-all-start.5 = ((bf16[8,64,768]{2,1,0:T(8,128)(2,1)}), bf16[8,64,768]{2,1,0:T(8,128)(2,1)}, u32[]{:S(2)}, u32[]{:S(2)}) async-start(bf16[8,64,768]{2,1,0:T(8,128)(2,1)} %bitcast.33), calls=%async_computation.5 | async-start | bytes 1572864 | tf_op jit(solution)/shard_map/all_to_all | solution.py:41
  236.4 7.8 %collective-permute-start.5 = (bf16[512,768]{1,0:T(8,128)(2,1)}, bf16[512,768]{1,0:T(8,128)(2,1)}, u32[]{:S(2)}, u32[]{:S(2)}) collective-permute-start(bf16[512,768]{1,0:T(8,128)(2,1)} %fusion.49), channel_id=1, source_target_pairs={{0,1},{1,0},{2,3},{3,2},{4,5},{5,4},{6,7},{7,6},{8,9},{9,8},{10,11... | collective-permute-start | bytes 2359304 | tf_op jit(solution)/shard_map/ppermute | solution.py:35
  244.1 31.0 %copy-start.5 = (f32[256,768]{1,0:T(8,128)S(1)}, f32[256,768]{1,0:T(8,128)}, u32[]{:S(2)}) copy-start(f32[256,768]{1,0:T(8,128)} %copy-done.4) | copy-start | bytes 2359300
  250.6 24.6 %all-to-all-start.4 = ((bf16[8,64,768]{2,1,0:T(8,128)(2,1)}), bf16[8,64,768]{2,1,0:T(8,128)(2,1)}, u32[]{:S(2)}, u32[]{:S(2)}) async-start(bf16[8,64,768]{2,1,0:T(8,128)(2,1)} %bitcast.187), calls=%async_computation.4 | async-start | bytes 1572864 | tf_op jit(solution)/shard_map/all_to_all | solution.py:41
  278.8 22.6 %copy-start.30 = (bf16[1,256,768]{2,1,0:T(8,128)(2,1)S(1)}, bf16[1,256,768]{2,1,0:T(8,128)(2,1)}, u32[]{:S(2)}) copy-start(bf16[1,256,768]{2,1,0:T(8,128)(2,1)} %param.18) | copy-start | bytes 1179652
  289.4 39.5 %copy-start.25 = (f32[512,1536]{1,0:T(8,128)S(1)}, f32[512,1536]{1,0:T(8,128)}, u32[]{:S(2)}) copy-start(f32[512,1536]{1,0:T(8,128)} %copy-done.24) | copy-start | bytes 9437188
  289.5 11.9 %collective-permute-start.7 = (bf16[256,768]{1,0:T(8,128)(2,1)S(1)}, bf16[256,768]{1,0:T(8,128)(2,1)S(1)}, u32[]{:S(2)}, u32[]{:S(2)}) collective-permute-start(bf16[256,768]{1,0:T(8,128)(2,1)S(1)} %convert_element_type.335), channel_id=1, source_target_pairs={{16,0},{17,1},{18,2},{19,3},{20,4},{21,5},{22,6},{23,7},{24,8},{25... | collective-permute-start | bytes 1179656 | tf_op jit(solution)/shard_map/ppermute | solution.py:31
  326.6 6.7 %copy-start.34 = (bf16[8,64,768]{2,1,0:T(8,128)(2,1)}, bf16[8,64,768]{2,1,0:T(8,128)(2,1)S(1)}, u32[]{:S(2)}) copy-start(bf16[8,64,768]{2,1,0:T(8,128)(2,1)S(1)} %all_to_all.52) | copy-start | bytes 2359300
  326.6 5.0 %copy-start.33 = (bf16[1,768,1536]{2,1,0:T(8,128)(2,1)S(1)}, bf16[1,768,1536]{2,1,0:T(8,128)(2,1)}, u32[]{:S(2)}) copy-start(bf16[1,768,1536]{2,1,0:T(8,128)(2,1)} %param.26) | copy-start | bytes 7077892
  326.6 2.3 collective-permute-start.8
  328.9 2.7 copy-start.39
  331.6 2.5 copy-start.32
  333.1 3.7 collective-permute-start.9
  336.8 2.3 copy-start.43
  339.1 24.9 %all-to-all-start.7 = ((bf16[8,64,768]{2,1,0:T(8,128)(2,1)}), bf16[8,64,768]{2,1,0:T(8,128)(2,1)}, u32[]{:S(2)}, u32[]{:S(2)}) async-start(bf16[8,64,768]{2,1,0:T(8,128)(2,1)} %bitcast.191), calls=%async_computation.7 | async-start | bytes 1572864 | tf_op jit(solution)/shard_map/all_to_all | solution.py:41
  386.2 5.5 %collective-permute-start.10 = (bf16[8,48,3072]{2,1,0:T(8,128)(2,1)}, bf16[8,48,3072]{2,1,0:T(8,128)(2,1)}, u32[]{:S(2)}, u32[]{:S(2)}) collective-permute-start(bf16[8,48,3072]{2,1,0:T(8,128)(2,1)} %dynamic-slice_bitcast_fusion), channel_id=1, source_target_pairs={{0,1},{1,0},{2,3},{3,2},{4,5},{5,4},{6,7},{7,6},{8,9},{9,8},{10,11... | collective-permute-start | bytes 7077896 | tf_op jit(solution)/shard_map/ppermute | solution.py:35
  387.6 12.0 %all-to-all-start.8 = ((f32[16,16,128]{2,1,0:T(8,128)}), f32[16,16,128]{2,1,0:T(8,128)S(1)}, u32[]{:S(2)}, u32[]{:S(2)}) async-start(f32[16,16,128]{2,1,0:T(8,128)} %pad.29), calls=%async_computation.8 | async-start | bytes 262144 | tf_op jit(solution)/shard_map/all_to_all | solution.py:454
  396.4 7.5 %copy-start.28 = (bf16[8,64,768]{2,1,0:T(8,128)(2,1)S(1)}, bf16[8,64,768]{2,1,0:T(8,128)(2,1)}, u32[]{:S(2)}) copy-start(bf16[8,64,768]{2,1,0:T(8,128)(2,1)} %all_to_all.51) | copy-start | bytes 2359300
  399.6 58.0 %all-to-all-start.9 = ((bf16[8,48,3072]{2,1,0:T(8,128)(2,1)}), bf16[8,48,3072]{2,1,0:T(8,128)(2,1)}, u32[]{:S(2)}, u32[]{:S(2)}) async-start(bf16[8,48,3072]{2,1,0:T(8,128)(2,1)} %fusion), calls=%async_computation.9 | async-start | bytes 4718592 | tf_op jit(solution)/shard_map/all_to_all | solution.py:41
  405.1 3.0 copy-start.26
  408.2 2.1 copy-start.44
  410.3 5.5 %copy-start.35 = (bf16[8,64,768]{2,1,0:T(8,128)(2,1)S(1)}, bf16[8,64,768]{2,1,0:T(8,128)(2,1)}, u32[]{:S(2)}) copy-start(bf16[8,64,768]{2,1,0:T(8,128)(2,1)} %copy-done.34) | copy-start | bytes 2359300
  410.3 5.5 %copy-start.40 = (bf16[512,768]{1,0:T(8,128)(2,1)S(1)}, bf16[512,768]{1,0:T(8,128)(2,1)}, u32[]{:S(2)}) copy-start(bf16[512,768]{1,0:T(8,128)(2,1)} %copy-done.39) | copy-start | bytes 2359300
  415.8 4.4 copy-start.3
  415.8 4.4 copy-start.18
  415.8 4.4 copy-start.27
  (16 other events, 15.9 us)
Sparse Core Ops, SparseCore 0:
  10.9 56.3 all-gather.1
